TPU v7x, 32 devices: a whole 2x2x4 slice. The times are simulated.
32 devices in a mesh: prow: 4 (over y, x), pcol: 8 (over z, core).
Axes of the slice: x: 2, y: 2, z: 4, core: 2. Of those that a mesh axis runs over, the one named last changes fastest.
Arguments:
- ainv: float32 [16384, 16384], P('prow', 'pcol'), as said below
- panels: float32 [3, 16384, 512], P(None, 'prow', 'pcol'), may hold values from -0.53 to 0.53
- pattern: int32 [3, 128], replicated, may hold values 0 or 1
- coupling: float32 [3, 512, 512], replicated, may hold values from -0.25 to 0.25
- dinv: float32 [3, 512, 512], replicated, as said below
Outputs:
- xpanel: float32 [3, 16384, 512], P(None, 'prow', 'pcol')
- xcross: float32 [3, 512, 512], P(None, 'pcol')
- ydiag: float32 [3, 512, 512], P(None, 'pcol')
Inputs may be any that keep to these rules, and one draw needn't show every extreme that they name: ainv is symmetric: ainv equals its transpose up to rounding. Each dinv[k] is symmetric: it equals its transpose exactly.
All inputs are finite; a program needn't handle non-finite values.
Results may differ from a plain program's by a relative error of at most 0.000092.
Values sent between devices are 32-bit elements; how exact they have to be, the bound alone decides.
No kernel may reach another device: no remote copies, remote signals or barrier semaphores. Data moves between devices by JAX's collectives and lax.ppermute only.
A program may use at most 192 MiB of HBM per device.

v0:
```python
import functools

import jax
import jax.numpy as jnp
from jax import lax
from jax.experimental import pallas as pl
from jax.experimental.pallas import tpu as pltpu
from jax.sharding import PartitionSpec as P

NB = 128
MIB = 1024 * 1024

precise = lax.Precision.HIGHEST


def matmul(left, right):
    return jnp.dot(left, right, precision=precise, preferred_element_type=jnp.float32)


def tdot(left, right):
    return lax.dot_general(
        left, right, (((0,), (0,)), ((), ())), precision=precise, preferred_element_type=jnp.float32
    )


def tile_of(size, wanted):
    return wanted if size % wanted == 0 else size


def split(values):
    high = lax.reduce_precision(values, exponent_bits=8, mantissa_bits=7)
    return high.astype(jnp.bfloat16), (values - high).astype(jnp.bfloat16)


def split_here(values):
    high = values.astype(jnp.bfloat16)
    return high, (values - high.astype(jnp.float32)).astype(jnp.bfloat16)


def triple_dot(left, right_high, right_low, contract=(1, 0)):
    dims = (((contract[0],), (contract[1],)), ((), ()))
    rows = left.shape[0] // 2
    wide = lax.dot_general(left, right_high, dims, preferred_element_type=jnp.float32)
    cross = lax.dot_general(left[:rows], right_low, dims, preferred_element_type=jnp.float32)
    return wide[:rows] + wide[rows:] + cross


def exchange(value, axis, size, step):
    return lax.ppermute(value, axis, [(i, i ^ step) for i in range(size)])


class Order:
    def __init__(self):
        self.last = None

    def __call__(self, kernel, operands, in_specs, out_shape, out_specs, grid, flops, moved,
                 name, scratch=(), limit=56, prefetch=(), extra=(), aliases=None):
        tokens = list(extra) + ([] if self.last is None else [self.last])
        skip = len(prefetch) + len(operands)

        def body(*refs):
            kernel(*refs[:skip], *refs[skip + len(tokens):])

        got = pl.pallas_call(
            body,
            out_shape=out_shape,
            grid_spec=pltpu.PrefetchScalarGridSpec(
                num_scalar_prefetch=len(prefetch),
                grid=grid,
                in_specs=list(in_specs) + [pl.BlockSpec(memory_space=pl.ANY)] * len(tokens),
                out_specs=out_specs,
                scratch_shapes=list(scratch),
            ),
            compiler_params=pltpu.CompilerParams(vmem_limit_bytes=limit * MIB),
            cost_estimate=pl.CostEstimate(
                flops=flops // 16, bytes_accessed=moved // 16, transcendentals=0
            ),
            input_output_aliases=aliases or {},
            name=name,
        )(*prefetch, *operands, *tokens)
        self.last = got[0] if isinstance(got, (tuple, list)) else got
        return got


def shape_of(shape, dtype=jnp.float32):
    return jax.ShapeDtypeStruct(shape, dtype)


def mask_kernel(panel_ref, mask_ref, out_ref):
    out_ref[...] = panel_ref[0] * mask_ref[0]


def masked(order, panels, mask, j, lo, hi, extra):
    rows = panels.shape[2]
    count = hi - lo
    return order(
        mask_kernel,
        [panels, mask],
        [
            pl.BlockSpec((1, count, rows), lambda i: (j, lo // count, 0)),
            pl.BlockSpec((1, 1, rows), lambda i: (j, 0, 0)),
        ],
        shape_of((count, rows)),
        pl.BlockSpec((count, rows), lambda i: (0, 0)),
        (1,),
        count * rows,
        8 * count * rows,
        "masked",
        extra=extra,
    )


def prepare_kernel(partner_ref, a_ref, high_ref, low_ref):
    high_ref[0], low_ref[0] = split_here(a_ref[...])


def prepared(order, ainv, partner, count, part):
    rows = ainv.shape[0]
    if part % 128:
        pieces = [
            split(lax.dynamic_slice_in_dim(ainv, partner[s] * part, part, 1)) for s in range(count)
        ]
        return jnp.stack([p[0] for p in pieces], 0), jnp.stack([p[1] for p in pieces], 0)
    tile = tile_of(rows, 1024)
    shape = shape_of((count, rows, part), jnp.bfloat16)
    spec = pl.BlockSpec((1, tile, part), lambda s, i, partner: (s, i, 0))
    return order(
        prepare_kernel,
        [ainv],
        [pl.BlockSpec((tile, part), lambda s, i, partner: (i, partner[s]))],
        (shape, shape),
        (spec, spec),
        (count, rows // tile),
        4 * ainv.size,
        8 * ainv.size,
        "prepared",
        prefetch=[partner],
    )


def product_kernel(count, steps, with_pre, with_split, *refs):
    refs = list(refs)
    s, k = pl.program_id(0), pl.program_id(1)
    if with_split:
        gathered_ref = refs.pop(0)
        pre_ref = refs.pop(0) if with_pre else None
        a_high_ref, a_low_ref = refs.pop(0), refs.pop(0)
        factor_ref = refs.pop(0)
        outer, strip, depth = gathered_ref.shape
        rows = outer * strip
        here = pl.ds(pl.multiple_of(k * depth, depth), depth)

        @pl.when(s == 0)
        def _():
            @pl.loop(0, outer)
            def _(i):
                first = pl.multiple_of(i * strip, strip)
                values = gathered_ref[i]
                if with_pre:
                    values = values - pre_ref[pl.ds(first, strip), :]
                high, low = split_here(values)
                factor_ref[pl.ds(first, strip), here] = high
                factor_ref[pl.ds(pl.multiple_of(first + rows, strip), strip), here] = low

        factor = factor_ref[:, here]
    else:
        factor_ref, a_high_ref, a_low_ref = refs[:3]
        refs = refs[3:]
        factor = factor_ref[...]
    outs, total_ref = refs[:count], refs[count]
    value = triple_dot(factor, a_high_ref[0], a_low_ref[0])

    @pl.when(k == 0)
    def _():
        total_ref[...] = value

    @pl.when(k > 0)
    def _():
        total_ref[...] += value

    for i in range(count):
        @pl.when((s == i) & (k == steps - 1))
        def _():
            outs[i][...] = total_ref[...]


def products(order, factor, inverse, first, last, pre=None, piece=(0, 1)):
    with_split = factor.dtype == jnp.float32
    a_high, a_low = inverse
    count = last - first
    part = a_high.shape[2]
    length = factor.shape[-1]
    if with_split:
        strip = factor.shape[1] // piece[1]
        rows = factor.shape[0] * strip
    else:
        rows = factor.shape[0] // 2
    depth = tile_of(length, 2048)
    steps = length // depth
    a_spec = pl.BlockSpec((1, depth, part), lambda s, k: (s + first, k, 0))
    out_shape = [shape_of((rows, part))] * count
    out_specs = [pl.BlockSpec((rows, part), lambda s, k: (0, 0))] * count
    if with_split:
        operands = [factor] + ([] if pre is None else [pre]) + [a_high, a_low]

        def once(k, s):
            return jnp.where(s == 0, k, steps - 1)

        in_specs = [
            pl.BlockSpec((factor.shape[0], strip, depth), lambda s, k: (0, piece[0], once(k, s))),
            pl.BlockSpec((rows, depth), lambda s, k: (0, once(k, s))),
        ][: len(operands) - 2] + [a_spec, a_spec]
        out_shape = [shape_of((2 * rows, length), jnp.bfloat16)] + out_shape
        out_specs = [pl.BlockSpec((2 * rows, length), lambda s, k: (0, 0))] + out_specs
    else:
        operands = [factor, a_high, a_low]
        in_specs = [pl.BlockSpec((2 * rows, depth), lambda s, k: (0, k)), a_spec, a_spec]
    got = order(
        functools.partial(product_kernel, count, steps, pre is not None, with_split),
        operands,
        in_specs,
        out_shape,
        out_specs,
        (count, steps),
        6 * rows * length * part * count,
        4 * length * part * count + 8 * rows * length,
        "products",
        scratch=[pltpu.VMEM((rows, part), jnp.float32)],
    )
    if with_split:
        return got[0], list(got[1:])
    return factor, list(got)


def elimination_kernel(sources, sizes, *refs):
    value = None
    for i in range(sources):
        coupled, factor_ref = refs[2 * i][...], refs[2 * i + 1]
        depth = factor_ref.shape[0] // 2
        term = triple_dot(coupled, factor_ref[:depth, :], factor_ref[depth:, :])
        value = term if value is None else value + term
    start = 0
    for ref, size in zip(refs[2 * sources :], sizes):
        ref[...] = value[start : start + size]
        start += size


def elimination(order, pairs, sizes, extra=()):
    operands = [value for pair in pairs for value in pair]
    rows, depth = pairs[0][0].shape[0] // 2, pairs[0][0].shape[1]
    length = pairs[0][1].shape[1]
    tile = tile_of(length, 512)
    left = pl.BlockSpec((2 * rows, depth), lambda i: (0, 0))
    right = pl.BlockSpec((2 * depth, tile), lambda i: (0, i))
    return order(
        functools.partial(elimination_kernel, len(pairs), sizes),
        operands,
        [left, right] * len(pairs),
        [shape_of((size, length)) for size in sizes],
        [pl.BlockSpec((size, tile), lambda i: (0, i)) for size in sizes],
        (length // tile,),
        6 * rows * depth * length * len(pairs),
        4 * length * (rows + depth * len(pairs)),
        "elimination",
        extra=extra,
    )


def sum_kernel(shares, *refs):
    out = refs[-1]
    start = 0
    for i in range(0, len(refs) - 1, shares):
        value = refs[i][...]
        for ref in refs[i + 1 : i + shares]:
            value = value + ref[...]
        out[0, start : start + value.shape[0], :] = -value
        start += value.shape[0]


def negative_sums(order, groups, cols_n):
    flat = [value for group in groups for value in group]
    width = flat[0].shape[1]
    counts = [group[0].shape[0] // cols_n for group in groups]
    shape = (cols_n, sum(counts), width)
    return order(
        functools.partial(sum_kernel, len(groups[0])),
        flat,
        [pl.BlockSpec((v.shape[0] // cols_n, width), lambda i: (i, 0)) for v in flat],
        shape_of(shape),
        pl.BlockSpec((1, sum(counts), width), lambda i: (i, 0, 0)),
        (cols_n,),
        sum(v.size for v in flat),
        4 * sum(v.size for v in flat),
        "negative_sums",
    )


def relay_kernel(*refs):
    start = 0
    for ref in refs[:-1]:
        refs[-1][:, start : start + ref.shape[1], :] = ref[...]
        start += ref.shape[1]


def relay(order, *values):
    outer, _, width = values[0].shape
    counts = [v.shape[1] for v in values]
    half = outer // 2
    return order(
        relay_kernel,
        list(values),
        [pl.BlockSpec((half, n, width), lambda i: (i, 0, 0)) for n in counts],
        shape_of((outer, sum(counts), width)),
        pl.BlockSpec((half, sum(counts), width), lambda i: (i, 0, 0)),
        (2,),
        sum(v.size for v in values),
        8 * sum(v.size for v in values),
        "relay",
    )


def assembly_kernel(in_ref, *refs):
    out_ref = refs[-1]
    outer, inner, _, part = in_ref.shape
    count = out_ref.shape[1]
    for i in range(out_ref.shape[0]):
        for a in range(inner):
            for q in range(outer):
                to = pl.ds((a * outer + q) * part, part)
                out_ref[i, :, to] = in_ref[q, a, i * count : (i + 1) * count, :]


def assembled(order, value, j, n, shape, whole=None):
    operands = [value] + ([] if whole is None else [whole])
    return order(
        assembly_kernel,
        operands,
        [pl.BlockSpec(value.shape, lambda i: (0, 0, 0, 0))]
        + [pl.BlockSpec(memory_space=pl.ANY)] * (len(operands) - 1),
        shape_of(shape),
        pl.BlockSpec((n, *shape[1:]), lambda i: (j, 0, 0)),
        (1,),
        value.size,
        8 * value.size,
        "assembled",
        aliases={} if whole is None else {1: 0},
    )


def inner_kernel(terms, *refs):
    out = refs[-1]

    @pl.when(pl.program_id(0) == 0)
    def _():
        out[...] = jnp.zeros_like(out)

    left = refs[0][...]
    left = -left.reshape(left.shape[0] * left.shape[1], left.shape[2])
    stacked = jnp.concatenate(split_here(left), 0)
    for right, (row, column, kept) in zip(refs[1:-1], terms):
        half = right.shape[0] // 2
        value = triple_dot(stacked, right[:half], right[half:], (1, 1))
        out[row : row + kept, column : column + half] += value[:kept]


def inner_products(order, whole, j, n, rights, terms, shape, extra=()):
    _, count, length = whole.shape
    depth = tile_of(length, 1024)
    return order(
        functools.partial(inner_kernel, terms),
        [whole] + list(rights),
        [pl.BlockSpec((n, count, depth), lambda k: (j, 0, k))]
        + [pl.BlockSpec((v.shape[0], depth), lambda k: (0, k)) for v in rights],
        shape_of(shape),
        pl.BlockSpec(shape, lambda k: (0, 0)),
        (length // depth,),
        6 * shape[0] * shape[1] * length,
        sum(2 * v.size for v in rights),
        "inner_products",
        extra=extra,
    )


def finish_kernel(shares, cols_n, sizes, *refs):
    def total(first):
        value = refs[first][...]
        for ref in refs[first + 1 : first + shares]:
            value = value + ref[...]
        return value

    one, two = (total(shares * i) for i in range(2))
    base_cross, base_diag, cross, diag, place = refs[2 * shares :]
    wide = sum(sizes)
    cut = cols_n * sizes[0]
    place[: 2 * wide, :] = one[3 * wide :]
    place[2 * wide :, :] = two

    def put(out, base, i, row):
        for c in range(cols_n):
            for start, first, size in ((0, 0, sizes[0]), (sizes[0], cut, sizes[1])):
                to = pl.ds(c * wide + start, size)
                out[i, :, to] = base[i, :, to] + place[row : row + wide, pl.ds(first + c * size, size)]

    diag[0] = base_diag[0] + one[:wide]
    cross[0] = base_cross[0] + one[wide : 2 * wide]
    diag[1] = base_diag[1] + one[2 * wide : 3 * wide]
    put(cross, base_cross, 1, 0)
    put(cross, base_cross, 2, wide)
    put(diag, base_diag, 2, 2 * wide)


def finish(order, one, two, base_cross, base_diag, cols_n, sizes):
    operands = one + two + [base_cross, base_diag]
    shape = base_cross.shape
    once = [pl.BlockSpec(v.shape, lambda i, n=v.ndim: (0,) * n) for v in operands]
    moved = 4 * sum(v.size for v in operands)
    return order(
        functools.partial(finish_kernel, len(one), cols_n, sizes),
        operands,
        once,
        [shape_of(shape)] * 2,
        [once[-1]] * 2,
        (1,),
        moved // 4,
        moved,
        "finish",
        scratch=[pltpu.VMEM((3 * shape[1], shape[2]), jnp.float32)],
    )


def shards(ainv, panels, pattern, coupling, dinv):
    rows_n = lax.axis_size("prow")
    cols_n = lax.axis_size("pcol")
    row = lax.axis_index("prow")
    col = lax.axis_index("pcol")
    local_rows, local_cols = panels.shape[1:]
    part = ainv.shape[1] // rows_n
    ratio = cols_n // rows_n
    blocks_here = local_rows // NB

    flags = lax.dynamic_slice_in_dim(pattern, row * blocks_here, blocks_here, 1)
    mask = jnp.repeat(flags.astype(jnp.float32), NB, axis=1)[:, None, :]
    turned = jnp.swapaxes(panels, 1, 2)

    cut = local_cols // 2
    last_cuts = [(0, cut), (cut, local_cols)]
    partner = row ^ jnp.arange(rows_n, dtype=jnp.int32)

    def columns(matrix, cuts):
        cube = matrix.reshape(matrix.shape[0], cols_n, local_cols)
        kept = [cube[:, :, lo:hi].reshape(matrix.shape[0], -1) for lo, hi in cuts]
        return jnp.concatenate(split(jnp.concatenate(kept, 1).T), 0)

    c_one = columns(coupling[0], [(0, local_cols)])
    c_two = columns(coupling[1], last_cuts)
    c_three = columns(coupling[2], last_cuts)

    def gather(shard):
        return lax.all_gather(shard, "pcol", axis=0, tiled=True).reshape(cols_n, *shard.shape)

    def send(pieces):
        return [exchange(p, "prow", rows_n, s + 1) for s, p in enumerate(pieces)]

    def to_columns(groups):
        return lax.all_to_all(negative_sums(order, groups, cols_n), "pcol", 0, 0)

    def to_rows(value):
        count = value.shape[1]
        value = value.reshape(rows_n, ratio * count, part)
        value = lax.all_to_all(value, "prow", 0, 0)
        return value.reshape(rows_n, ratio, count, part)

    def share(value):
        return [value] + [exchange(value, "prow", rows_n, s) for s in range(1, rows_n)]

    first, second, third = coupling[0], coupling[1], coupling[2]
    start = col * local_cols

    def own_rows(matrix):
        return lax.dynamic_slice_in_dim(matrix, start, local_cols, 0)

    def own_cols(matrix):
        return lax.dynamic_slice_in_dim(matrix, start, local_cols, 1)

    bridge = second - matmul(first, third)
    d0 = own_rows(dinv[0])
    d1 = own_rows(dinv[1])
    k0 = tdot(own_cols(first), dinv[0])
    k1 = tdot(own_cols(bridge), dinv[0])
    k2 = tdot(own_cols(third), dinv[1])
    base_cross = jnp.stack(
        [-matmul(d0, first), -matmul(d0, bridge), matmul(k0, bridge) - matmul(d1, third)], 0
    )
    base_diag = jnp.stack(
        [d0, d1 + matmul(k0, first), own_rows(dinv[2]) + matmul(k1, bridge) + matmul(k2, third)], 0
    )

    order = Order()
    shard = masked(order, turned, mask, 0, 0, local_cols, [])
    g0 = gather(shard)
    inverse = prepared(order, ainv, partner, rows_n, part)

    early_work = [c_one, c_two, c_three, base_cross, base_diag]
    early_work = [c_one, c_two, c_three, base_cross, base_diag]
    early_work = [c_one, c_two, c_three, base_cross, base_diag]
    shard = masked(order, turned, mask, 1, 0, local_cols, [g0] + early_work)
    g1 = gather(shard)
    f0, sent = products(order, g0, inverse, 0, rows_n)
    s0 = [sent[0]] + send(sent[1:])
    pre1 = elimination(order, [(c_one, f0)], [cols_n * local_cols])

    shard = masked(order, turned, mask, 2, 0, local_cols, [g1])
    g2 = gather(shard)
    f1, sent = products(order, g1, inverse, 0, rows_n, pre1[0])
    s1 = [sent[0]] + send(sent[1:])
    pre2 = elimination(
        order, [(c_two, f0), (c_three, f1)], [cols_n * (hi - lo) for lo, hi in last_cuts], s0[1:]
    )
    m01 = to_columns([s0, s1])

    f2, sent = products(order, g2, inverse, 0, rows_n, pre2[0], (0, 2))
    s2 = [sent[0]] + send(sent[1:])
    f3, sent = products(order, g2, inverse, 1, rows_n, pre2[1], (1, 2))
    s3 = send(sent)
    m2 = to_columns([s2])
    _, own3 = products(order, f3, inverse, 0, 1)
    m01 = to_rows(relay(order, m01))
    m3 = to_columns([own3 + s3])
    whole = assembled(order, m01, 0, 2, turned.shape)
    m23 = to_rows(relay(order, m2, m3))
    columns_n, begin, pair = cols_n * local_cols, cols_n * cut, 2 * local_cols
    one = inner_products(
        order, whole, 0, 2, [f0, f1, f2, f3],
        [(0, 0, local_cols), (local_cols, 0, pair)]
        + [(local_cols + pair, c, pair) for c in (0, begin)],
        (local_cols + 2 * pair, columns_n),
    )
    one = share(one)
    whole = assembled(order, m23, 2, 1, turned.shape, whole)
    two = inner_products(
        order, whole, 2, 1, [f2, f3], [(0, c, local_cols) for c in (0, begin)],
        (local_cols, columns_n), one[1:],
    )
    two = share(two)
    cross, diag = finish(
        order, one, two, base_cross, base_diag, cols_n, (cut, local_cols - cut)
    )
    return (jnp.swapaxes(whole, 1, 2), cross, diag)


def solution(mesh):
    placed = (P("prow", "pcol"), P(None, "prow", "pcol"), P(), P(), P())
    return jax.shard_map(
        shards,
        mesh=mesh,
        in_specs=placed,
        out_specs=(P(None, "prow", "pcol"), P(None, "pcol", None), P(None, "pcol", None)),
        check_vma=False,
    )
```

profile of v0, /device:TPU:0, one launch (start us, length us, event | category | flops | bytes accessed | tf_op | source)
XLA Modules:
  0.0 520.5 jit_solution(3423348551868194869)
XLA Ops:
  8.8 2.3 masked.3.refs_2_
  11.2 1.8 fusion.43
  13.0 2.5 copy.18
  15.5 2.6 copy.17
  18.1 2.6 copy.16
  21.2 28.8 %prepared.1 = (bf16[4,4096,512]{2,1,0:T(8,128)(2,1)}, bf16[4,4096,512]{2,1,0:T(8,128)(2,1)}) custom-call(s32[4]{0:T(128)} %iota_xor_fusion.refs_0_, f32[4096,2048]{1,0:T(8,128)} %refs_1_.1, f32[64,4096]{1,0:T(8,128)} %masked.3.refs_2_), custom_call_target="tpu_custom_call" | custom-call | flops 2097152 | bytes 4194304 | tf_op jit(solution)/shard_map/prepared/pallas_call | solution.py:64
  51.3 1.9 convolution_subtract_fusion
  53.2 1.1 fusion.3
  55.9 1.1 fusion.46
  59.2 1.1 convolution_add_fusion.1
  62.6 1.1 pad_maximum_fusion.2.refs_5_.refs_2_
  63.8 1.5 pad_maximum_fusion
  65.3 30.7 %all-gather.4.cloned.1.call-done = f32[512,4096]{1,0:T(8,128)} async-done(((f32[64,4096]{1,0:T(8,128)}), f32[512,4096]{1,0:T(8,128)}) %all-gather.4.cloned.1.call-update) | async-done | bytes 8388624 | tf_op jit(solution)/shard_map/all_gather | solution.py:459
  96.0 2.3 masked.4.refs_3_
  98.6 38.1 %products.5 = (bf16[1024,4096]{1,0:T(8,128)(2,1)}, f32[512,512]{1,0:T(8,128)}, f32[512,512]{1,0:T(8,128)}, f32[512,512]{1,0:T(8,128)}, f32[512,512]{1,0:T(8,128)}) custom-call(f32[8,64,4096]{2,1,0:T(8,128)} %bitcast.100, bf16[4,4096,512]{2,1,0:T(8,128)(2,1)} %get-tuple-element.28.refs_8_.refs_1_.refs_2_, ...), custom_call_target="tpu_custom_call" | custom-call | flops 1610612736 | bytes 3145728 | tf_op jit(solution)/shard_map/products/pallas_call | solution.py:64
  136.7 12.5 %elimination.2.refs_3_.refs_1_ = f32[512,4096]{1,0:T(8,128)} custom-call(bf16[1024,512]{1,0:T(8,128)(2,1)} %get-tuple-element.69.refs_3_.refs_0_, bf16[1024,4096]{1,0:T(8,128)(2,1)} %get-tuple-element.30.refs_1_.refs_2_, bf16[1024,4096]{1,0:T(8,128)(2,1)} %get-tuple-element.30.refs_1_.refs_2_), custom_call_target="tpu_custom_call" | custom-call | flops 402653184 | bytes 1048576 | tf_op jit(solution)/shard_map/elimination/pallas_call | solution.py:64
  149.2 29.9 %all-gather.6.cloned.1.call-done = f32[512,4096]{1,0:T(8,128)} async-done(((f32[64,4096]{1,0:T(8,128)}), f32[512,4096]{1,0:T(8,128)}) %all-gather.6.cloned.1.call-update) | async-done | bytes 8388624 | tf_op jit(solution)/shard_map/all_gather | solution.py:459
  179.1 2.4 masked.5.refs_4_
  181.5 1.6 collective-permute-start
  183.1 1.5 collective-permute-start.1
  185.1 41.0 %products.6 = (bf16[1024,4096]{1,0:T(8,128)(2,1)}, f32[512,512]{1,0:T(8,128)}, f32[512,512]{1,0:T(8,128)}, f32[512,512]{1,0:T(8,128)}, f32[512,512]{1,0:T(8,128)}) custom-call(f32[8,64,4096]{2,1,0:T(8,128)} %bitcast.98, f32[512,4096]{1,0:T(8,128)} %elimination.2.refs_3_.refs_1_, bf16[4,4096,512]{2,1,0:T(8,128)(2,1)} %get-tuple-element.28.refs_8_.refs_1_.refs_2_, ...), custom_call_target="tpu_custom_call" | custom-call | flops 1610612736 | bytes 3145728 | tf_op jit(solution)/shard_map/products/pallas_call | solution.py:64
  226.1 1.2 collective-permute-start.3
  227.3 1.5 collective-permute-start.4
  229.6 1.5 collective-permute-done.1.refs_5_.refs_2_
  232.5 17.9 %elimination.3 = (f32[256,4096]{1,0:T(8,128)}, f32[256,4096]{1,0:T(8,128)}) custom-call(bf16[1024,512]{1,0:T(8,128)(2,1)} %get-tuple-element.70.refs_4_.refs_0_, bf16[1024,4096]{1,0:T(8,128)(2,1)} %get-tuple-element.30.refs_1_.refs_2_, bf16[1024,512]{1,0:T(8,128)(2,1)} %pad_maximum_fusion.2.refs_5_.refs_2_, ...), custom_call_target="tpu_custom_call" | custom-call | flops 805306368 | bytes 1572864 | tf_op jit(solution)/shard_map/elimination/pallas_call | solution.py:64
  250.4 2.2 collective-permute-done.3.refs_5_
  252.6 23.2 %collective-permute-done.4.refs_6_ = f32[512,512]{1,0:T(8,128)S(1)} collective-permute-done((f32[512,512]{1,0:T(8,128)}, f32[512,512]{1,0:T(8,128)S(1)}, u32[]{:S(2)}, u32[]{:S(2)}) %collective-permute-start.4) | collective-permute-done | bytes 1048608 | tf_op jit(solution)/shard_map/ppermute | solution.py:49
  275.8 1.0 copy-done.17
  277.2 7.0 %negative_sums.3.refs_4_ = f32[8,128,512]{2,1,0:T(8,128)} custom-call(f32[512,512]{1,0:T(8,128)} %get-tuple-element.36.refs_0_, f32[512,512]{1,0:T(8,128)} %copy-done.8, f32[512,512]{1,0:T(8,128)} %copy-done.9, f32[512,512]{1,0:T(8,128)} %copy-done.10, f32[512,512]{1,0:T(8,128)} %get-tuple-element.37.refs_4_, f32[512,512]{1,0:T(8,128)} %copy-done.16, ...), custom_call_target="tpu_custom_call" | custom-call | flops 131072 | bytes 524288 | tf_op jit(solution)/shard_map/negative_sums/pallas_call | solution.py:64
  284.1 3.6 all-to-all-start.1
  287.8 23.6 %products.7 = (bf16[512,4096]{1,0:T(8,128)(2,1)}, f32[256,512]{1,0:T(8,128)}, f32[256,512]{1,0:T(8,128)}, f32[256,512]{1,0:T(8,128)}, f32[256,512]{1,0:T(8,128)}) custom-call(f32[8,64,4096]{2,1,0:T(8,128)} %bitcast.101, f32[256,4096]{1,0:T(8,128)} %get-tuple-element.35.refs_8_.refs_1_, bf16[4,4096,512]{2,1,0:T(8,128)(2,1)} %get-tuple-element.28.refs_8_.refs_1_.refs_2_, ...), custom_call_target="tpu_custom_call" | custom-call | flops 805306368 | bytes 2621440 | tf_op jit(solution)/shard_map/products/pallas_call | solution.py:64
  312.0 1.5 collective-permute-start.7
  313.5 1.5 collective-permute-start.8
  314.9 19.3 %products.8 = (bf16[512,4096]{1,0:T(8,128)(2,1)}, f32[256,512]{1,0:T(8,128)}, f32[256,512]{1,0:T(8,128)}, f32[256,512]{1,0:T(8,128)}) custom-call(f32[8,64,4096]{2,1,0:T(8,128)} %bitcast.102, f32[256,4096]{1,0:T(8,128)} %get-tuple-element.45.refs_1_, bf16[4,4096,512]{2,1,0:T(8,128)(2,1)} %get-tuple-element.28.refs_8_.refs_1_.refs_2_, ...), custom_call_target="tpu_custom_call" | custom-call | flops 603979776 | bytes 2097152 | tf_op jit(solution)/shard_map/products/pallas_call | solution.py:64
  334.2 2.2 collective-permute-done.7.refs_2_
  336.5 1.5 collective-permute-done.8.refs_3_
  338.7 5.2 %negative_sums.4.refs_3_ = f32[8,32,512]{2,1,0:T(8,128)} custom-call(f32[256,512]{1,0:T(8,128)} %get-tuple-element.41.refs_0_, f32[256,512]{1,0:T(8,128)} %copy-done.22, f32[256,512]{1,0:T(8,128)} %copy-done.23, f32[256,512]{1,0:T(8,128)} %copy-done.24, bf16[512,4096]{1,0:T(8,128)(2,1)} %get-tuple-element.47.refs_4_.refs_0_.refs_2_), custom_call_target="tpu_custom_call" | custom-call | flops 32768 | bytes 131072 | tf_op jit(solution)/shard_map/negative_sums/pallas_call | solution.py:64
  344.0 4.8 all-to-all-start
  348.8 7.5 %products.9.refs_1_.refs_0_ = f32[256,512]{1,0:T(8,128)} custom-call(bf16[512,4096]{1,0:T(8,128)(2,1)} %get-tuple-element.47.refs_4_.refs_0_.refs_2_, bf16[4,4096,512]{2,1,0:T(8,128)(2,1)} %get-tuple-element.28.refs_8_.refs_1_.refs_2_, bf16[4,4096,512]{2,1,0:T(8,128)(2,1)} %get-tuple-element.29.refs_2_.refs_3_, f32[8,32,512]{2,1,0:T(8,128)} %negative_sums.4.refs_3_), custom_call_target="tpu_custom_call" | custom-call | flops 201326592 | bytes 1048576 | tf_op jit(solution)/shard_map/products/pallas_call | solution.py:64
  356.2 2.6 relay.2.refs_4_
  358.8 5.3 %all-to-all-done.refs_0_ = f32[8,32,512]{2,1,0:T(8,128)S(1)} async-done(((f32[8,32,512]{2,1,0:T(8,128)}), f32[8,32,512]{2,1,0:T(8,128)S(1)}, u32[]{:S(2)}, u32[]{:S(2)}) %all-to-all-start) | async-done | bytes 524320 | tf_op jit(solution)/shard_map/all_to_all | solution.py:465
  364.1 3.6 all-to-all-start.3
  367.7 2.0 collective-permute-start.9
  369.7 1.5 collective-permute-start.10
  371.3 33.9 %collective-permute-done.9.refs_1_ = f32[256,512]{1,0:T(8,128)S(1)} collective-permute-done((f32[256,512]{1,0:T(8,128)}, f32[256,512]{1,0:T(8,128)S(1)}, u32[]{:S(2)}, u32[]{:S(2)}) %collective-permute-start.9) | collective-permute-done | bytes 524320 | tf_op jit(solution)/shard_map/ppermute | solution.py:49
  405.2 10.8 %collective-permute-done.11.refs_3_ = f32[256,512]{1,0:T(8,128)S(1)} collective-permute-done((f32[256,512]{1,0:T(8,128)S(1)}, f32[256,512]{1,0:T(8,128)S(1)}, u32[]{:S(2)}, u32[]{:S(2)}) %collective-permute-start.11) | collective-permute-done | bytes 524320 | tf_op jit(solution)/shard_map/ppermute | solution.py:49
  416.8 5.2 %negative_sums.5.refs_1_ = f32[8,32,512]{2,1,0:T(8,128)} custom-call(f32[256,512]{1,0:T(8,128)} %products.9.refs_1_.refs_0_, f32[256,512]{1,0:T(8,128)} %copy-done.19, f32[256,512]{1,0:T(8,128)} %copy-done.20, f32[256,512]{1,0:T(8,128)} %copy-done.21, f32[8,128,512]{2,1,0:T(8,128)} %relay.2.refs_4_), custom_call_target="tpu_custom_call" | custom-call | flops 32768 | bytes 131072 | tf_op jit(solution)/shard_map/negative_sums/pallas_call | solution.py:64
  422.1 3.5 all-to-all-start.2
  425.6 3.0 assembled.2.refs_2_.refs_0_.refs_1_
  428.6 12.2 %all-to-all-done.2.refs_1_ = f32[8,32,512]{2,1,0:T(8,128)S(1)} async-done(((f32[8,32,512]{2,1,0:T(8,128)}), f32[8,32,512]{2,1,0:T(8,128)S(1)}, u32[]{:S(2)}, u32[]{:S(2)}) %all-to-all-start.2) | async-done | bytes 524320 | tf_op jit(solution)/shard_map/all_to_all | solution.py:465
  441.7 2.0 relay.3.refs_5_
  443.7 3.7 all-to-all-start.4
  447.5 13.0 %inner_products.2.refs_2_.refs_0_ = f32[320,512]{1,0:T(8,128)} custom-call(f32[3,64,4096]{2,1,0:T(8,128)} %assembled.2.refs_2_.refs_0_.refs_1_, bf16[1024,4096]{1,0:T(8,128)(2,1)} %get-tuple-element.30.refs_1_.refs_2_, bf16[1024,4096]{1,0:T(8,128)(2,1)} %get-tuple-element.31.refs_3_.refs_7_.refs_2_, ...), custom_call_target="tpu_custom_call" | custom-call | flops 251658240 | bytes 1572864 | tf_op jit(solution)/shard_map/inner_products/pallas_call | solution.py:64
  460.5 2.6 collective-permute-start.14
  464.0 1.0 copy-done.7
  464.9 2.3 assembled.3.refs_0_.refs_6_
  467.2 12.1 %collective-permute-done.14.refs_5_.refs_3_ = f32[320,512]{1,0:T(8,128)S(1)} collective-permute-done((f32[320,512]{1,0:T(8,128)}, f32[320,512]{1,0:T(8,128)S(1)}, u32[]{:S(2)}, u32[]{:S(2)}) %collective-permute-start.14) | collective-permute-done | bytes 655392 | tf_op jit(solution)/shard_map/ppermute | solution.py:49
  479.3 12.6 %collective-permute-done.13.refs_4_.refs_2_ = f32[320,512]{1,0:T(8,128)S(1)} collective-permute-done((f32[320,512]{1,0:T(8,128)}, f32[320,512]{1,0:T(8,128)S(1)}, u32[]{:S(2)}, u32[]{:S(2)}) %collective-permute-start.13) | collective-permute-done | bytes 655392 | tf_op jit(solution)/shard_map/ppermute | solution.py:49
  493.6 6.5 %inner_products.3.refs_4_.refs_10_ = f32[64,512]{1,0:T(8,128)} custom-call(f32[3,64,4096]{2,1,0:T(8,128)} %assembled.3.refs_0_.refs_6_, bf16[512,4096]{1,0:T(8,128)(2,1)} %get-tuple-element.46.refs_4_.refs_3_.refs_1_, bf16[512,4096]{1,0:T(8,128)(2,1)} %get-tuple-element.47.refs_4_.refs_0_.refs_2_, f32[320,512]{1,0:T(8,128)} %copy-done.13, ...), custom_call_target="tpu_custom_call" | custom-call | flops 50331648 | bytes 524288 | tf_op jit(solution)/shard_map/inner_products/pallas_call | solution.py:64
  500.1 1.7 collective-permute-start.17
  501.8 1.2 collective-permute-start.16
  503.5 4.0 collective-permute-done.17.refs_7_
  507.6 1.8 collective-permute-done.16.refs_6_
  510.7 3.3 finish.1
  (102 shorter events, 20.3 us)
Async XLA Ops:
  7.2 4.0 copy-start
  7.2 88.9 %all-gather.4.cloned.1.call-start = ((), (), s32[]{:S(2)}) async-start(), calls=%async_computation.5 | async-start | bytes 9437184 | tf_op jit(solution)/shard_map/all_gather | solution.py:459
  11.1 168.0 %all-gather.6.cloned.1.call-start = ((), (), s32[]{:S(2)}) async-start(), calls=%async_computation.6 | async-start | bytes 9437184 | tf_op jit(solution)/shard_map/all_gather | solution.py:459
  21.2 28.9 %copy-start.1 = (f32[3,512,512]{2,1,0:T(8,128)S(1)}, f32[3,512,512]{2,1,0:T(8,128)}, u32[]{:S(2)}) copy-start(f32[3,512,512]{2,1,0:T(8,128)} %param.9) | copy-start | bytes 9437188
  50.0 1.3 copy-start.2
  50.4 3.9 copy-start.5
  54.3 4.1 copy-start.6
  98.3 189.4 %all-gather.8.cloned.1.call-start = ((), (), s32[]{:S(2)}) async-start(), calls=%async_computation.7 | async-start | bytes 9437184 | tf_op jit(solution)/shard_map/all_gather | solution.py:459
  179.1 2.4 copy-start.29
  179.1 5.5 %copy-start.28 = (f32[512,512]{1,0:T(8,128)S(1)}, f32[512,512]{1,0:T(8,128)}, u32[]{:S(2)}) copy-start(f32[512,512]{1,0:T(8,128)} %get-tuple-element.34) | copy-start | bytes 3145732
  181.5 47.3 %collective-permute-start = (f32[512,512]{1,0:T(8,128)S(1)}, f32[512,512]{1,0:T(8,128)S(1)}, u32[]{:S(2)}, u32[]{:S(2)}) collective-permute-start(f32[512,512]{1,0:T(8,128)S(1)} %copy-done.29), channel_id=1, source_target_pairs={{0,8},{8,0},{16,24},{24,16},{1,9},{9,1},{17,25},{25,17},{2,10},{10... | collective-permute-start | bytes 3145736 | tf_op jit(solution)/shard_map/ppermute | solution.py:49
  183.1 48.0 %collective-permute-start.1 = (f32[512,512]{1,0:T(8,128)}, f32[512,512]{1,0:T(8,128)S(1)}, u32[]{:S(2)}, u32[]{:S(2)}) collective-permute-start(f32[512,512]{1,0:T(8,128)} %get-tuple-element.33), channel_id=1, source_target_pairs={{0,16},{8,24},{16,0},{24,8},{1,17},{9,25},{17,1},{25,9},{2,18},{10... | collective-permute-start | bytes 3145736 | tf_op jit(solution)/shard_map/ppermute | solution.py:49
  184.6 46.6 %collective-permute-start.2 = (f32[512,512]{1,0:T(8,128)S(1)}, f32[512,512]{1,0:T(8,128)S(1)}, u32[]{:S(2)}, u32[]{:S(2)}) collective-permute-start(f32[512,512]{1,0:T(8,128)S(1)} %copy-done.28), channel_id=1, source_target_pairs={{0,24},{8,16},{16,8},{24,0},{1,25},{9,17},{17,9},{25,1},{2,26},{10... | collective-permute-start | bytes 3145736 | tf_op jit(solution)/shard_map/ppermute | solution.py:49
  226.1 26.5 %collective-permute-start.3 = (f32[512,512]{1,0:T(8,128)}, f32[512,512]{1,0:T(8,128)S(1)}, u32[]{:S(2)}, u32[]{:S(2)}) collective-permute-start(f32[512,512]{1,0:T(8,128)} %get-tuple-element.38), channel_id=1, source_target_pairs={{0,8},{8,0},{16,24},{24,16},{1,9},{9,1},{17,25},{25,17},{2,10},{10... | collective-permute-start | bytes 3145736 | tf_op jit(solution)/shard_map/ppermute | solution.py:49
  227.3 48.4 %collective-permute-start.4 = (f32[512,512]{1,0:T(8,128)}, f32[512,512]{1,0:T(8,128)S(1)}, u32[]{:S(2)}, u32[]{:S(2)}) collective-permute-start(f32[512,512]{1,0:T(8,128)} %get-tuple-element.39), channel_id=1, source_target_pairs={{0,16},{8,24},{16,0},{24,8},{1,17},{9,25},{17,1},{25,9},{2,18},{10... | collective-permute-start | bytes 3145736 | tf_op jit(solution)/shard_map/ppermute | solution.py:49
  228.8 2.4 copy-start.8
  228.8 47.0 %collective-permute-start.5 = (f32[512,512]{1,0:T(8,128)}, f32[512,512]{1,0:T(8,128)S(1)}, u32[]{:S(2)}, u32[]{:S(2)}) collective-permute-start(f32[512,512]{1,0:T(8,128)} %get-tuple-element.40), channel_id=1, source_target_pairs={{0,24},{8,16},{16,8},{24,0},{1,25},{9,17},{17,9},{25,1},{2,26},{10... | collective-permute-start | bytes 3145736 | tf_op jit(solution)/shard_map/ppermute | solution.py:49
  231.2 1.0 copy-start.9
  231.2 1.3 copy-start.10
  252.6 23.2 %copy-start.16 = (f32[512,512]{1,0:T(8,128)}, f32[512,512]{1,0:T(8,128)S(1)}, u32[]{:S(2)}) copy-start(f32[512,512]{1,0:T(8,128)S(1)} %collective-permute-done.3.refs_5_) | copy-start | bytes 3145732
  275.8 1.1 copy-start.17
  275.8 1.4 copy-start.18
  284.1 59.9 %all-to-all-start.1 = ((f32[8,128,512]{2,1,0:T(8,128)}), f32[8,128,512]{2,1,0:T(8,128)S(1)}, u32[]{:S(2)}, u32[]{:S(2)}) async-start(f32[8,128,512]{2,1,0:T(8,128)} %negative_sums.3.refs_4_), calls=%async_computation.1 | async-start | bytes 4194304 | tf_op jit(solution)/shard_map/all_to_all | solution.py:465
  311.4 22.8 %collective-permute-start.6 = (f32[256,512]{1,0:T(8,128)}, f32[256,512]{1,0:T(8,128)S(1)}, u32[]{:S(2)}, u32[]{:S(2)}) collective-permute-start(f32[256,512]{1,0:T(8,128)} %get-tuple-element.42), channel_id=1, source_target_pairs={{0,8},{8,0},{16,24},{24,16},{1,9},{9,1},{17,25},{25,17},{2,10},{10... | collective-permute-start | bytes 1572872 | tf_op jit(solution)/shard_map/ppermute | solution.py:49
  312.0 24.5 %collective-permute-start.7 = (f32[256,512]{1,0:T(8,128)}, f32[256,512]{1,0:T(8,128)S(1)}, u32[]{:S(2)}, u32[]{:S(2)}) collective-permute-start(f32[256,512]{1,0:T(8,128)} %get-tuple-element.43), channel_id=1, source_target_pairs={{0,16},{8,24},{16,0},{24,8},{1,17},{9,25},{17,1},{25,9},{2,18},{10... | collective-permute-start | bytes 1572872 | tf_op jit(solution)/shard_map/ppermute | solution.py:49
  313.5 24.5 %collective-permute-start.8 = (f32[256,512]{1,0:T(8,128)}, f32[256,512]{1,0:T(8,128)S(1)}, u32[]{:S(2)}, u32[]{:S(2)}) collective-permute-start(f32[256,512]{1,0:T(8,128)} %get-tuple-element.44), channel_id=1, source_target_pairs={{0,24},{8,16},{16,8},{24,0},{1,25},{9,17},{17,9},{25,1},{2,26},{10... | collective-permute-start | bytes 1572872 | tf_op jit(solution)/shard_map/ppermute | solution.py:49
  334.2 3.7 copy-start.22
  336.5 1.5 copy-start.23
  338.0 0.8 copy-start.24
  344.0 12.2 %copy-start.3 = (f32[8,128,512]{2,1,0:T(8,128)}, f32[8,128,512]{2,1,0:T(8,128)S(1)}, u32[]{:S(2)}) copy-start(f32[8,128,512]{2,1,0:T(8,128)S(1)} %all-to-all-done.1.refs_0_) | copy-start | bytes 6291460
  344.0 20.1 %all-to-all-start = ((f32[8,32,512]{2,1,0:T(8,128)}), f32[8,32,512]{2,1,0:T(8,128)S(1)}, u32[]{:S(2)}, u32[]{:S(2)}) async-start(f32[8,32,512]{2,1,0:T(8,128)} %negative_sums.4.refs_3_), calls=%async_computation | async-start | bytes 1048576 | tf_op jit(solution)/shard_map/all_to_all | solution.py:465
  358.8 12.4 %copy-start.30 = (f32[256,512]{1,0:T(8,128)S(1)}, f32[256,512]{1,0:T(8,128)}, u32[]{:S(2)}) copy-start(f32[256,512]{1,0:T(8,128)} %get-tuple-element.50) | copy-start | bytes 1572868
  364.1 57.9 %copy-start.14 = (f32[8,32,512]{2,1,0:T(8,128)}, f32[8,32,512]{2,1,0:T(8,128)S(1)}, u32[]{:S(2)}) copy-start(f32[8,32,512]{2,1,0:T(8,128)S(1)} %all-to-all-done.refs_0_) | copy-start | bytes 1572868
  364.1 57.9 %all-to-all-start.3 = ((f32[4,256,512]{2,1,0:T(8,128)}), f32[4,256,512]{2,1,0:T(8,128)S(1)}, u32[]{:S(2)}, u32[]{:S(2)}) async-start(f32[4,256,512]{2,1,0:T(8,128)} %bitcast.106), calls=%async_computation.3 | async-start | bytes 4194304 | tf_op jit(solution)/shard_map/all_to_all | solution.py:470
  367.7 37.5 %collective-permute-start.9 = (f32[256,512]{1,0:T(8,128)}, f32[256,512]{1,0:T(8,128)S(1)}, u32[]{:S(2)}, u32[]{:S(2)}) collective-permute-start(f32[256,512]{1,0:T(8,128)} %get-tuple-element.48), channel_id=1, source_target_pairs={{0,8},{8,0},{16,24},{24,16},{1,9},{9,1},{17,25},{25,17},{2,10},{10... | collective-permute-start | bytes 1572872 | tf_op jit(solution)/shard_map/ppermute | solution.py:49
  369.7 35.5 %collective-permute-start.10 = (f32[256,512]{1,0:T(8,128)}, f32[256,512]{1,0:T(8,128)S(1)}, u32[]{:S(2)}, u32[]{:S(2)}) collective-permute-start(f32[256,512]{1,0:T(8,128)} %get-tuple-element.49), channel_id=1, source_target_pairs={{0,16},{8,24},{16,0},{24,8},{1,17},{9,25},{17,1},{25,9},{2,18},{10... | collective-permute-start | bytes 1572872 | tf_op jit(solution)/shard_map/ppermute | solution.py:49
  371.2 44.8 %collective-permute-start.11 = (f32[256,512]{1,0:T(8,128)S(1)}, f32[256,512]{1,0:T(8,128)S(1)}, u32[]{:S(2)}, u32[]{:S(2)}) collective-permute-start(f32[256,512]{1,0:T(8,128)S(1)} %copy-done.30), channel_id=1, source_target_pairs={{0,24},{8,16},{16,8},{24,0},{1,25},{9,17},{17,9},{25,1},{2,26},{10... | collective-permute-start | bytes 1572872 | tf_op jit(solution)/shard_map/ppermute | solution.py:49
  405.2 10.8 %copy-start.19 = (f32[256,512]{1,0:T(8,128)}, f32[256,512]{1,0:T(8,128)S(1)}, u32[]{:S(2)}) copy-start(f32[256,512]{1,0:T(8,128)S(1)} %collective-permute-done.9.refs_1_) | copy-start | bytes 1572868
  405.2 10.8 %copy-start.20 = (f32[256,512]{1,0:T(8,128)}, f32[256,512]{1,0:T(8,128)S(1)}, u32[]{:S(2)}) copy-start(f32[256,512]{1,0:T(8,128)S(1)} %collective-permute-done.10.refs_2_) | copy-start | bytes 1572868
  416.0 0.8 copy-start.21
  422.0 3.5 copy-start.4
  422.1 18.8 %all-to-all-start.2 = ((f32[8,32,512]{2,1,0:T(8,128)}), f32[8,32,512]{2,1,0:T(8,128)S(1)}, u32[]{:S(2)}, u32[]{:S(2)}) async-start(f32[8,32,512]{2,1,0:T(8,128)} %negative_sums.5.refs_1_), calls=%async_computation.2 | async-start | bytes 1048576 | tf_op jit(solution)/shard_map/all_to_all | solution.py:465
  440.8 0.8 copy-start.15
  443.7 20.2 %all-to-all-start.4 = ((f32[4,128,512]{2,1,0:T(8,128)}), f32[4,128,512]{2,1,0:T(8,128)S(1)}, u32[]{:S(2)}, u32[]{:S(2)}) async-start(f32[4,128,512]{2,1,0:T(8,128)} %bitcast.107), calls=%async_computation.4 | async-start | bytes 2097152 | tf_op jit(solution)/shard_map/all_to_all | solution.py:470
  460.5 18.8 %collective-permute-start.14 = (f32[320,512]{1,0:T(8,128)}, f32[320,512]{1,0:T(8,128)S(1)}, u32[]{:S(2)}, u32[]{:S(2)}) collective-permute-start(f32[320,512]{1,0:T(8,128)} %inner_products.2.refs_2_.refs_0_), channel_id=1, source_target_pairs={{0,24},{8,16},{16,8},{24,0},{1,25},{9,17},{17,9},{25,1},{2,26},{10... | collective-permute-start | bytes 1966088 | tf_op jit(solution)/shard_map/ppermute | solution.py:49
  463.1 28.8 %collective-permute-start.13 = (f32[320,512]{1,0:T(8,128)}, f32[320,512]{1,0:T(8,128)S(1)}, u32[]{:S(2)}, u32[]{:S(2)}) collective-permute-start(f32[320,512]{1,0:T(8,128)} %inner_products.2.refs_2_.refs_0_), channel_id=1, source_target_pairs={{0,16},{8,24},{16,0},{24,8},{1,17},{9,25},{17,1},{25,9},{2,18},{10... | collective-permute-start | bytes 1966088 | tf_op jit(solution)/shard_map/ppermute | solution.py:49
  463.7 28.3 %collective-permute-start.12 = (f32[320,512]{1,0:T(8,128)}, f32[320,512]{1,0:T(8,128)S(1)}, u32[]{:S(2)}, u32[]{:S(2)}) collective-permute-start(f32[320,512]{1,0:T(8,128)} %inner_products.2.refs_2_.refs_0_), channel_id=1, source_target_pairs={{0,8},{8,0},{16,24},{24,16},{1,9},{9,1},{17,25},{25,17},{2,10},{10... | collective-permute-start | bytes 1966088 | tf_op jit(solution)/shard_map/ppermute | solution.py:49
  464.0 1.0 copy-start.7
  479.3 12.7 %copy-start.11 = (f32[320,512]{1,0:T(8,128)}, f32[320,512]{1,0:T(8,128)S(1)}, u32[]{:S(2)}) copy-start(f32[320,512]{1,0:T(8,128)S(1)} %collective-permute-done.14.refs_5_.refs_3_) | copy-start | bytes 1966084
  491.9 0.9 copy-start.12
  492.7 0.8 copy-start.13
  500.1 7.5 %collective-permute-start.17 = (f32[64,512]{1,0:T(8,128)}, f32[64,512]{1,0:T(8,128)S(1)}, u32[]{:S(2)}, u32[]{:S(2)}) collective-permute-start(f32[64,512]{1,0:T(8,128)} %inner_products.3.refs_4_.refs_10_), channel_id=1, source_target_pairs={{0,24},{8,16},{16,8},{24,0},{1,25},{9,17},{17,9},{25,1},{2,26},{10... | collective-permute-start | bytes 393224 | tf_op jit(solution)/shard_map/ppermute | solution.py:49
  501.8 7.6 %collective-permute-start.16 = (f32[64,512]{1,0:T(8,128)}, f32[64,512]{1,0:T(8,128)S(1)}, u32[]{:S(2)}, u32[]{:S(2)}) collective-permute-start(f32[64,512]{1,0:T(8,128)} %inner_products.3.refs_4_.refs_10_), channel_id=1, source_target_pairs={{0,16},{8,24},{16,0},{24,8},{1,17},{9,25},{17,1},{25,9},{2,18},{10... | collective-permute-start | bytes 393224 | tf_op jit(solution)/shard_map/ppermute | solution.py:49
  503.0 6.4 %collective-permute-start.15 = (f32[64,512]{1,0:T(8,128)}, f32[64,512]{1,0:T(8,128)S(1)}, u32[]{:S(2)}, u32[]{:S(2)}) collective-permute-start(f32[64,512]{1,0:T(8,128)} %inner_products.3.refs_4_.refs_10_), channel_id=1, source_target_pairs={{0,8},{8,0},{16,24},{24,16},{1,9},{9,1},{17,25},{25,17},{2,10},{10... | collective-permute-start | bytes 393224 | tf_op jit(solution)/shard_map/ppermute | solution.py:49
  507.6 1.8 copy-start.25
  509.4 0.6 copy-start.26
  510.0 0.6 copy-start.27
Sparse Core Ops, SparseCore 0:
  11.3 84.7 all-gather.3
  98.5 80.5 all-gather.5
  181.7 80.5 all-gather.7
where the time goes:
time: 523 us; the launch traced here: 520 us
  Pallas kernels  246 us (47%)
  waiting for transfers between devices  184 us (35%)
  starting transfers between devices  40.6 us (8%)
  local copies, waits for them, and re-layouts  19.8 us (4%)
  between operations  14 us (3%)
  matrix products  10.5 us (2%)
  other arithmetic  5.43 us (1%)
    pallas_call x21, Pallas kernels, __call__(): pl.pallas_call(body, out_shape=out_shape, grid_spec=pltpu.PrefetchScalarG...  246 us
    ppermute x18, waiting for transfers between devices, exchange(): return lax.ppermute(value, axis, [(i, i ^ step) for i in range(size)])  106 us
    all_gather x3, waiting for transfers between devices, gather(): lax.all_gather(shard, 'pcol', axis=0, tiled=True)  60.7 us
    ppermute x18, starting transfers between devices, exchange(): return lax.ppermute(value, axis, [(i, i ^ step) for i in range(size)])  21.1 us
    all_to_all x3, waiting for transfers between devices, to_columns(): return lax.all_to_all(negative_sums(order, groups, cols_n), 'pcol', 0, 0)  17.5 us
    unnamed x65, local copies, waits for them, and re-layouts  16.9 us
    all_to_all x3, starting transfers between devices, to_columns(): return lax.all_to_all(negative_sums(order, groups, cols_n), 'pcol', 0, 0)  11.9 us
  transfers between devices with their start and end apart: 26, of which 15 were waited for; matrix products, arithmetic and copies ran while one was open for 5% of the time, Pallas kernels for 44%

commit v1 on v0

--- a/solution.py
+++ b/solution.py
@@ -388,8 +388,8 @@
             value = value + ref[...]
         return value
 
-    one, two = (total(shares * i) for i in range(2))
-    base_cross, base_diag, cross, diag, place = refs[2 * shares :]
+    one, two = -refs[0][...], total(1)
+    base_cross, base_diag, cross, diag, place = refs[1 + shares :]
     wide = sum(sizes)
     cut = cols_n * sizes[0]
     place[: 2 * wide, :] = one[3 * wide :]
@@ -410,12 +410,12 @@
 
 
 def finish(order, one, two, base_cross, base_diag, cols_n, sizes):
-    operands = one + two + [base_cross, base_diag]
+    operands = [one] + two + [base_cross, base_diag]
     shape = base_cross.shape
     once = [pl.BlockSpec(v.shape, lambda i, n=v.ndim: (0,) * n) for v in operands]
     moved = 4 * sum(v.size for v in operands)
     return order(
-        functools.partial(finish_kernel, len(one), cols_n, sizes),
+        functools.partial(finish_kernel, len(two), cols_n, sizes),
         operands,
         once,
         [shape_of(shape)] * 2,
@@ -514,20 +514,20 @@
     f1, sent = products(order, g1, inverse, 0, rows_n, pre1[0])
     s1 = [sent[0]] + send(sent[1:])
     pre2 = elimination(
-        order, [(c_two, f0), (c_three, f1)], [cols_n * (hi - lo) for lo, hi in last_cuts], s0[1:]
-    )
-    m01 = to_columns([s0, s1])
+        order, [(c_two, f0), (c_three, f1)], [cols_n * (hi - lo) for lo, hi in last_cuts]
+    )
 
     f2, sent = products(order, g2, inverse, 0, rows_n, pre2[0], (0, 2))
     s2 = [sent[0]] + send(sent[1:])
+    m01 = to_columns([s0, s1])
     f3, sent = products(order, g2, inverse, 1, rows_n, pre2[1], (1, 2))
     s3 = send(sent)
     m2 = to_columns([s2])
     _, own3 = products(order, f3, inverse, 0, 1)
+    m3 = to_columns([own3 + s3])
     m01 = to_rows(relay(order, m01))
-    m3 = to_columns([own3 + s3])
+    m23 = to_rows(relay(order, m2, m3))
     whole = assembled(order, m01, 0, 2, turned.shape)
-    m23 = to_rows(relay(order, m2, m3))
     columns_n, begin, pair = cols_n * local_cols, cols_n * cut, 2 * local_cols
     one = inner_products(
         order, whole, 0, 2, [f0, f1, f2, f3],
@@ -539,9 +539,10 @@
     whole = assembled(order, m23, 2, 1, turned.shape, whole)
     two = inner_products(
         order, whole, 2, 1, [f2, f3], [(0, c, local_cols) for c in (0, begin)],
-        (local_cols, columns_n), one[1:],
+        (local_cols, columns_n),
     )
     two = share(two)
+    one = negative_sums(order, [one], 1)[0]
     cross, diag = finish(
         order, one, two, base_cross, base_diag, cols_n, (cut, local_cols - cut)
     )

time: 523 us -> 510 us (0.975)
  waiting for transfers between devices: 184 us -> 158 us
  blocking collectives: 0 us -> 19.6 us
    ppermute x18, waiting for transfers between devices: 106 us -> 30.6 us  [exchange(): return lax.ppermute(value, axis, [(i, i ^ step) for i in range(size)])]
    all_to_all x2, waiting for transfers between devices: 0.01 us -> 22.7 us  [to_rows(): value = lax.all_to_all(value, 'prow', 0, 0)]
    all_to_all x0 -> x1, blocking collectives: none -> 19.6 us  [to_columns(): return lax.all_to_all(negative_sums(order, groups, cols_n), 'pcol', 0, 0)]
    all_gather x3, waiting for transfers between devices: 60.7 us -> 75.4 us  [gather(): lax.all_gather(shard, 'pcol', axis=0, tiled=True)]
    all_to_all x3 -> x2, waiting for transfers between devices: 17.5 us -> 28.8 us  [to_columns(): return lax.all_to_all(negative_sums(order, groups, cols_n), 'pcol', 0, 0)]
    all_to_all x3 -> x2, starting transfers between devices: 11.9 us -> 7.1 us  [to_columns(): return lax.all_to_all(negative_sums(order, groups, cols_n), 'pcol', 0, 0)]
    unnamed x65 -> x55, local copies, waits for them, and re-layouts: 16.9 us -> 12.5 us
    pallas_call x21 -> x22, Pallas kernels: 246 us -> 248 us  [__call__(): pl.pallas_call(body, out_shape=out_shape, grid_spec=pltpu.PrefetchScalarG...]
  transfers between devices with their start and end apart: 26 -> 25, of which waited for: 15 -> 12; matrix products, arithmetic and copies ran while one was open for 5% -> 5% of each run, Pallas kernels for 44% -> 46%
where the time goes in v1:
time: 510 us; the launch traced here: 508 us
  Pallas kernels  248 us (49%)
  waiting for transfers between devices  158 us (31%)
  starting transfers between devices  37.4 us (7%)
  blocking collectives  19.6 us (4%)
  local copies, waits for them, and re-layouts  15.4 us (3%)
  between operations  14 us (3%)
  matrix products  10.5 us (2%)
  other arithmetic  5.45 us (1%)
    pallas_call x22, Pallas kernels, __call__(): pl.pallas_call(body, out_shape=out_shape, grid_spec=pltpu.PrefetchScalarG...  248 us
    all_gather x3, waiting for transfers between devices, gather(): lax.all_gather(shard, 'pcol', axis=0, tiled=True)  75.4 us
    ppermute x18, waiting for transfers between devices, exchange(): return lax.ppermute(value, axis, [(i, i ^ step) for i in range(size)])  30.6 us
    all_to_all x2, waiting for transfers between devices, to_columns(): return lax.all_to_all(negative_sums(order, groups, cols_n), 'pcol', 0, 0)  28.8 us
    all_to_all x2, waiting for transfers between devices, to_rows(): value = lax.all_to_all(value, 'prow', 0, 0)  22.7 us
    ppermute x18, starting transfers between devices, exchange(): return lax.ppermute(value, axis, [(i, i ^ step) for i in range(size)])  22.6 us
    all_to_all x1, blocking collectives, to_columns(): return lax.all_to_all(negative_sums(order, groups, cols_n), 'pcol', 0, 0)  19.6 us
    unnamed x55, local copies, waits for them, and re-layouts  12.5 us
  transfers between devices with their start and end apart: 25, of which 12 were waited for; matrix products, arithmetic and copies ran while one was open for 5% of the time, Pallas kernels for 46%

profile of v1, /device:TPU:0, one launch (start us, length us, event | category | flops | bytes accessed | tf_op | source)
XLA Modules:
  0.0 507.7 jit_solution(7855186697502009635)
XLA Ops:
  7.2 0.9 dynamic-slice_convert_fusion
  8.8 2.3 masked.3.refs_2_
  11.2 1.8 fusion.43
  13.0 2.6 copy.18
  15.5 2.6 copy.17
  18.1 2.5 copy.16
  21.2 28.8 %prepared.1 = (bf16[4,4096,512]{2,1,0:T(8,128)(2,1)}, bf16[4,4096,512]{2,1,0:T(8,128)(2,1)}) custom-call(s32[4]{0:T(128)} %iota_xor_fusion.refs_0_, f32[4096,2048]{1,0:T(8,128)} %refs_1_.1, f32[64,4096]{1,0:T(8,128)} %masked.3.refs_2_), custom_call_target="tpu_custom_call" | custom-call | flops 2097152 | bytes 4194304 | tf_op jit(solution)/shard_map/prepared/pallas_call | solution.py:64
  51.3 1.9 convolution_subtract_fusion
  53.2 1.1 fusion.3
  55.9 1.1 fusion.46
  59.2 1.1 convolution_add_fusion.1
  61.1 0.9 pad_maximum_fusion.3
  62.6 1.1 pad_maximum_fusion.2.refs_5_.refs_2_
  63.9 1.5 pad_maximum_fusion
  65.3 30.7 %all-gather.4.cloned.1.call-done = f32[512,4096]{1,0:T(8,128)} async-done(((f32[64,4096]{1,0:T(8,128)}), f32[512,4096]{1,0:T(8,128)}) %all-gather.4.cloned.1.call-update) | async-done | bytes 8388624 | tf_op jit(solution)/shard_map/all_gather | solution.py:459
  96.0 2.3 masked.4.refs_3_
  98.6 38.0 %products.5 = (bf16[1024,4096]{1,0:T(8,128)(2,1)}, f32[512,512]{1,0:T(8,128)}, f32[512,512]{1,0:T(8,128)}, f32[512,512]{1,0:T(8,128)}, f32[512,512]{1,0:T(8,128)}) custom-call(f32[8,64,4096]{2,1,0:T(8,128)} %bitcast.101, bf16[4,4096,512]{2,1,0:T(8,128)(2,1)} %get-tuple-element.28.refs_8_.refs_1_.refs_2_, ...), custom_call_target="tpu_custom_call" | custom-call | flops 1610612736 | bytes 3145728 | tf_op jit(solution)/shard_map/products/pallas_call | solution.py:64
  136.6 12.5 %elimination.2.refs_3_.refs_1_ = f32[512,4096]{1,0:T(8,128)} custom-call(bf16[1024,512]{1,0:T(8,128)(2,1)} %get-tuple-element.69.refs_3_.refs_0_, bf16[1024,4096]{1,0:T(8,128)(2,1)} %get-tuple-element.30.refs_1_.refs_2_, bf16[1024,4096]{1,0:T(8,128)(2,1)} %get-tuple-element.30.refs_1_.refs_2_), custom_call_target="tpu_custom_call" | custom-call | flops 402653184 | bytes 1048576 | tf_op jit(solution)/shard_map/elimination/pallas_call | solution.py:64
  149.1 30.0 %all-gather.6.cloned.1.call-done = f32[512,4096]{1,0:T(8,128)} async-done(((f32[64,4096]{1,0:T(8,128)}), f32[512,4096]{1,0:T(8,128)}) %all-gather.6.cloned.1.call-update) | async-done | bytes 8388624 | tf_op jit(solution)/shard_map/all_gather | solution.py:459
  179.1 2.3 masked.5.refs_4_
  181.4 1.6 collective-permute-start.3
  183.0 1.5 collective-permute-start.4
  184.9 41.0 %products.6 = (bf16[1024,4096]{1,0:T(8,128)(2,1)}, f32[512,512]{1,0:T(8,128)}, f32[512,512]{1,0:T(8,128)}, f32[512,512]{1,0:T(8,128)}, f32[512,512]{1,0:T(8,128)}) custom-call(f32[8,64,4096]{2,1,0:T(8,128)} %bitcast.99, f32[512,4096]{1,0:T(8,128)} %elimination.2.refs_3_.refs_1_, bf16[4,4096,512]{2,1,0:T(8,128)(2,1)} %get-tuple-element.28.refs_8_.refs_1_.refs_2_, ...), custom_call_target="tpu_custom_call" | custom-call | flops 1610612736 | bytes 3145728 | tf_op jit(solution)/shard_map/products/pallas_call | solution.py:64
  226.0 1.2 collective-permute-start.6
  227.1 1.5 collective-permute-start.7
  229.4 17.9 %elimination.3 = (f32[256,4096]{1,0:T(8,128)}, f32[256,4096]{1,0:T(8,128)}) custom-call(bf16[1024,512]{1,0:T(8,128)(2,1)} %get-tuple-element.70.refs_4_.refs_0_, bf16[1024,4096]{1,0:T(8,128)(2,1)} %get-tuple-element.30.refs_1_.refs_2_, bf16[1024,512]{1,0:T(8,128)(2,1)} %pad_maximum_fusion.2.refs_5_.refs_2_, ...), custom_call_target="tpu_custom_call" | custom-call | flops 805306368 | bytes 1572864 | tf_op jit(solution)/shard_map/elimination/pallas_call | solution.py:64
  247.4 14.8 %all-gather.8.cloned.1.call-done = f32[512,4096]{1,0:T(8,128)} async-done(((f32[64,4096]{1,0:T(8,128)}), f32[512,4096]{1,0:T(8,128)}) %all-gather.8.cloned.1.call-update) | async-done | bytes 8388624 | tf_op jit(solution)/shard_map/all_gather | solution.py:459
  262.1 23.5 %products.7 = (bf16[512,4096]{1,0:T(8,128)(2,1)}, f32[256,512]{1,0:T(8,128)}, f32[256,512]{1,0:T(8,128)}, f32[256,512]{1,0:T(8,128)}, f32[256,512]{1,0:T(8,128)}) custom-call(f32[8,64,4096]{2,1,0:T(8,128)} %bitcast.102, f32[256,4096]{1,0:T(8,128)} %get-tuple-element.32.refs_1_.refs_4_, bf16[4,4096,512]{2,1,0:T(8,128)(2,1)} %get-tuple-element.28.refs_8_.refs_1_.refs_2_, ...), custom_call_target="tpu_custom_call" | custom-call | flops 805306368 | bytes 2621440 | tf_op jit(solution)/shard_map/products/pallas_call | solution.py:64
  285.6 1.6 collective-permute-start
  287.2 1.5 collective-permute-start.1
  289.2 7.0 %negative_sums.4.refs_4_ = f32[8,128,512]{2,1,0:T(8,128)} custom-call(f32[512,512]{1,0:T(8,128)} %get-tuple-element.38.refs_0_, f32[512,512]{1,0:T(8,128)} %copy-done.9, f32[512,512]{1,0:T(8,128)} %copy-done.10, f32[512,512]{1,0:T(8,128)} %copy-done.11, f32[512,512]{1,0:T(8,128)} %get-tuple-element.42.refs_4_, f32[512,512]{1,0:T(8,128)} %collective-permute-done.6.refs_5_, ...), custom_call_target="tpu_custom_call" | custom-call | flops 131072 | bytes 524288 | tf_op jit(solution)/shard_map/negative_sums/pallas_call | solution.py:64
  296.2 19.2 %products.8 = (bf16[512,4096]{1,0:T(8,128)(2,1)}, f32[256,512]{1,0:T(8,128)}, f32[256,512]{1,0:T(8,128)}, f32[256,512]{1,0:T(8,128)}) custom-call(f32[8,64,4096]{2,1,0:T(8,128)} %bitcast.103, f32[256,4096]{1,0:T(8,128)} %get-tuple-element.37.refs_1_, bf16[4,4096,512]{2,1,0:T(8,128)(2,1)} %get-tuple-element.28.refs_8_.refs_1_.refs_2_, ...), custom_call_target="tpu_custom_call" | custom-call | flops 603979776 | bytes 2097152 | tf_op jit(solution)/shard_map/products/pallas_call | solution.py:64
  316.5 5.2 %negative_sums.5.refs_3_ = f32[8,32,512]{2,1,0:T(8,128)} custom-call(f32[256,512]{1,0:T(8,128)} %get-tuple-element.33.refs_0_, f32[256,512]{1,0:T(8,128)} %copy-done.18, f32[256,512]{1,0:T(8,128)} %copy-done.19, f32[256,512]{1,0:T(8,128)} %copy-done.20, bf16[512,4096]{1,0:T(8,128)(2,1)} %get-tuple-element.47.refs_4_.refs_0_.refs_2_), custom_call_target="tpu_custom_call" | custom-call | flops 32768 | bytes 131072 | tf_op jit(solution)/shard_map/negative_sums/pallas_call | solution.py:64
  321.8 19.6 %all_to_all.25.refs_0_ = f32[8,32,512]{2,1,0:T(8,128)} all-to-all(f32[8,32,512]{2,1,0:T(8,128)} %negative_sums.5.refs_3_), channel_id=1, replica_groups=mesh['prow'=4,'pcol'=8] {'pcol'}, dimensions={0} | all-to-all | bytes 1048576 | tf_op jit(solution)/shard_map/all_to_all | solution.py:465
  341.4 3.6 all-to-all-start.2
  345.0 1.6 collective-permute-start.9
  346.6 1.5 collective-permute-start.10
  348.6 7.5 %products.9.refs_0_.refs_4_ = f32[256,512]{1,0:T(8,128)} custom-call(bf16[512,4096]{1,0:T(8,128)(2,1)} %get-tuple-element.47.refs_4_.refs_0_.refs_2_, bf16[4,4096,512]{2,1,0:T(8,128)(2,1)} %get-tuple-element.28.refs_8_.refs_1_.refs_2_, bf16[4,4096,512]{2,1,0:T(8,128)(2,1)} %get-tuple-element.29.refs_2_.refs_3_, f32[8,32,512]{2,1,0:T(8,128)} %negative_sums.5.refs_3_), custom_call_target="tpu_custom_call" | custom-call | flops 201326592 | bytes 1048576 | tf_op jit(solution)/shard_map/products/pallas_call | solution.py:64
  356.1 4.0 collective-permute-done.9.refs_1_
  360.0 10.7 %collective-permute-done.10.refs_2_ = f32[256,512]{1,0:T(8,128)S(1)} collective-permute-done((f32[256,512]{1,0:T(8,128)S(1)}, f32[256,512]{1,0:T(8,128)S(1)}, u32[]{:S(2)}, u32[]{:S(2)}) %collective-permute-start.10) | collective-permute-done | bytes 524320 | tf_op jit(solution)/shard_map/ppermute | solution.py:49
  370.7 1.0 collective-permute-done.11.refs_3_
  371.7 0.8 copy-done.17
  372.5 5.3 %negative_sums.6.refs_1_ = f32[8,32,512]{2,1,0:T(8,128)} custom-call(f32[256,512]{1,0:T(8,128)} %products.9.refs_0_.refs_4_, f32[256,512]{1,0:T(8,128)} %copy-done.15, f32[256,512]{1,0:T(8,128)} %copy-done.16, f32[256,512]{1,0:T(8,128)} %copy-done.17, f32[256,512]{1,0:T(8,128)} %products.9.refs_0_.refs_4_), custom_call_target="tpu_custom_call" | custom-call | flops 32768 | bytes 131072 | tf_op jit(solution)/shard_map/negative_sums/pallas_call | solution.py:64
  377.8 16.2 %all-to-all-done.2.refs_0_ = f32[8,128,512]{2,1,0:T(8,128)S(1)} async-done(((f32[8,128,512]{2,1,0:T(8,128)}), f32[8,128,512]{2,1,0:T(8,128)S(1)}, u32[]{:S(2)}, u32[]{:S(2)}) %all-to-all-start.2) | async-done | bytes 2097184 | tf_op jit(solution)/shard_map/all_to_all | solution.py:465
  394.0 3.5 all-to-all-start.1
  397.5 2.6 relay.2.refs_2_
  400.1 12.7 %all-to-all-done.1.refs_1_ = f32[8,32,512]{2,1,0:T(8,128)S(1)} async-done(((f32[8,32,512]{2,1,0:T(8,128)}), f32[8,32,512]{2,1,0:T(8,128)S(1)}, u32[]{:S(2)}, u32[]{:S(2)}) %all-to-all-start.1) | async-done | bytes 524320 | tf_op jit(solution)/shard_map/all_to_all | solution.py:465
  412.8 3.7 all-to-all-start.4
  416.5 2.1 relay.3.refs_1_
  418.6 22.7 %all-to-all-done.4 = f32[4,256,512]{2,1,0:T(8,128)S(1)} async-done(((f32[4,256,512]{2,1,0:T(8,128)}), f32[4,256,512]{2,1,0:T(8,128)S(1)}, u32[]{:S(2)}, u32[]{:S(2)}) %all-to-all-start.4) | async-done | bytes 2097184 | tf_op jit(solution)/shard_map/all_to_all | solution.py:470
  441.3 3.7 all-to-all-start.3
  445.1 3.0 assembled.2.refs_0_.refs_5_.refs_1_
  448.1 13.0 %inner_products.2.refs_2_.refs_0_ = f32[320,512]{1,0:T(8,128)} custom-call(f32[3,64,4096]{2,1,0:T(8,128)} %assembled.2.refs_0_.refs_5_.refs_1_, bf16[1024,4096]{1,0:T(8,128)(2,1)} %get-tuple-element.30.refs_1_.refs_2_, bf16[1024,4096]{1,0:T(8,128)(2,1)} %get-tuple-element.31.refs_3_.refs_4_.refs_2_, ...), custom_call_target="tpu_custom_call" | custom-call | flops 251658240 | bytes 1572864 | tf_op jit(solution)/shard_map/inner_products/pallas_call | solution.py:64
  461.1 2.7 collective-permute-start.14
  464.6 1.0 copy-done.7
  465.6 2.3 assembled.3.refs_0_.refs_3_
  467.9 6.5 %inner_products.3.refs_4_.refs_1_ = f32[64,512]{1,0:T(8,128)} custom-call(f32[3,64,4096]{2,1,0:T(8,128)} %assembled.3.refs_0_.refs_3_, bf16[512,4096]{1,0:T(8,128)(2,1)} %get-tuple-element.46.refs_8_.refs_3_.refs_1_, bf16[512,4096]{1,0:T(8,128)(2,1)} %get-tuple-element.47.refs_4_.refs_0_.refs_2_, f32[3,64,4096]{2,1,0:T(8,128)} %assembled.3.refs_0_.refs_3_), custom_call_target="tpu_custom_call" | custom-call | flops 50331648 | bytes 524288 | tf_op jit(solution)/shard_map/inner_products/pallas_call | solution.py:64
  474.3 2.7 collective-permute-start.17
  477.6 2.4 collective-permute-done.14.refs_3_
  479.9 1.7 collective-permute-start.15
  481.6 11.8 %collective-permute-done.13.refs_2_ = f32[320,512]{1,0:T(8,128)S(1)} collective-permute-done((f32[320,512]{1,0:T(8,128)}, f32[320,512]{1,0:T(8,128)S(1)}, u32[]{:S(2)}, u32[]{:S(2)}) %collective-permute-start.13) | collective-permute-done | bytes 655392 | tf_op jit(solution)/shard_map/ppermute | solution.py:49
  494.2 0.8 copy-done.14
  495.1 2.7 negative_sums.7.refs_7_
  498.5 2.7 finish.1
  (92 shorter events, 14.5 us)
Async XLA Ops:
  7.2 4.0 copy-start
  7.2 88.9 %all-gather.4.cloned.1.call-start = ((), (), s32[]{:S(2)}) async-start(), calls=%async_computation.5 | async-start | bytes 9437184 | tf_op jit(solution)/shard_map/all_gather | solution.py:459
  11.1 168.0 %all-gather.6.cloned.1.call-start = ((), (), s32[]{:S(2)}) async-start(), calls=%async_computation.6 | async-start | bytes 9437184 | tf_op jit(solution)/shard_map/all_gather | solution.py:459
  21.2 28.8 %copy-start.1 = (f32[3,512,512]{2,1,0:T(8,128)S(1)}, f32[3,512,512]{2,1,0:T(8,128)}, u32[]{:S(2)}) copy-start(f32[3,512,512]{2,1,0:T(8,128)} %param.9) | copy-start | bytes 9437188
  50.0 1.3 copy-start.2
  50.4 4.0 copy-start.5
  54.3 4.1 copy-start.6
  98.3 163.8 %all-gather.8.cloned.1.call-start = ((), (), s32[]{:S(2)}) async-start(), calls=%async_computation.7 | async-start | bytes 9437184 | tf_op jit(solution)/shard_map/all_gather | solution.py:459
  181.4 47.2 %collective-permute-start.3 = (f32[512,512]{1,0:T(8,128)}, f32[512,512]{1,0:T(8,128)S(1)}, u32[]{:S(2)}, u32[]{:S(2)}) collective-permute-start(f32[512,512]{1,0:T(8,128)} %get-tuple-element.39), channel_id=1, source_target_pairs={{0,8},{8,0},{16,24},{24,16},{1,9},{9,1},{17,25},{25,17},{2,10},{10... | collective-permute-start | bytes 3145736 | tf_op jit(solution)/shard_map/ppermute | solution.py:49
  183.0 102.6 %collective-permute-start.4 = (f32[512,512]{1,0:T(8,128)}, f32[512,512]{1,0:T(8,128)S(1)}, u32[]{:S(2)}, u32[]{:S(2)}) collective-permute-start(f32[512,512]{1,0:T(8,128)} %get-tuple-element.40), channel_id=1, source_target_pairs={{0,16},{8,24},{16,0},{24,8},{1,17},{9,25},{17,1},{25,9},{2,18},{10... | collective-permute-start | bytes 3145736 | tf_op jit(solution)/shard_map/ppermute | solution.py:49
  184.4 102.8 %collective-permute-start.5 = (f32[512,512]{1,0:T(8,128)}, f32[512,512]{1,0:T(8,128)S(1)}, u32[]{:S(2)}, u32[]{:S(2)}) collective-permute-start(f32[512,512]{1,0:T(8,128)} %get-tuple-element.41), channel_id=1, source_target_pairs={{0,24},{8,16},{16,8},{24,0},{1,25},{9,17},{17,9},{25,1},{2,26},{10... | collective-permute-start | bytes 3145736 | tf_op jit(solution)/shard_map/ppermute | solution.py:49
  226.0 62.7 %collective-permute-start.6 = (f32[512,512]{1,0:T(8,128)}, f32[512,512]{1,0:T(8,128)}, u32[]{:S(2)}, u32[]{:S(2)}) collective-permute-start(f32[512,512]{1,0:T(8,128)} %get-tuple-element.43), channel_id=1, source_target_pairs={{0,8},{8,0},{16,24},{24,16},{1,9},{9,1},{17,25},{25,17},{2,10},{10... | collective-permute-start | bytes 3145736 | tf_op jit(solution)/shard_map/ppermute | solution.py:49
  227.1 62.0 %collective-permute-start.7 = (f32[512,512]{1,0:T(8,128)}, f32[512,512]{1,0:T(8,128)}, u32[]{:S(2)}, u32[]{:S(2)}) collective-permute-start(f32[512,512]{1,0:T(8,128)} %get-tuple-element.44), channel_id=1, source_target_pairs={{0,16},{8,24},{16,0},{24,8},{1,17},{9,25},{17,1},{25,9},{2,18},{10... | collective-permute-start | bytes 3145736 | tf_op jit(solution)/shard_map/ppermute | solution.py:49
  228.6 18.8 %copy-start.9 = (f32[512,512]{1,0:T(8,128)}, f32[512,512]{1,0:T(8,128)S(1)}, u32[]{:S(2)}) copy-start(f32[512,512]{1,0:T(8,128)S(1)} %collective-permute-done.3.refs_1_) | copy-start | bytes 3145732
  228.6 60.6 %collective-permute-start.8 = (f32[512,512]{1,0:T(8,128)}, f32[512,512]{1,0:T(8,128)}, u32[]{:S(2)}, u32[]{:S(2)}) collective-permute-start(f32[512,512]{1,0:T(8,128)} %get-tuple-element.45), channel_id=1, source_target_pairs={{0,24},{8,16},{16,8},{24,0},{1,25},{9,17},{17,9},{25,1},{2,26},{10... | collective-permute-start | bytes 3145736 | tf_op jit(solution)/shard_map/ppermute | solution.py:49
  285.6 3.6 copy-start.10
  285.6 29.7 %collective-permute-start = (f32[256,512]{1,0:T(8,128)}, f32[256,512]{1,0:T(8,128)S(1)}, u32[]{:S(2)}, u32[]{:S(2)}) collective-permute-start(f32[256,512]{1,0:T(8,128)} %get-tuple-element.34), channel_id=1, source_target_pairs={{0,8},{8,0},{16,24},{24,16},{1,9},{9,1},{17,25},{25,17},{2,10},{10... | collective-permute-start | bytes 1572872 | tf_op jit(solution)/shard_map/ppermute | solution.py:49
  287.2 2.0 copy-start.11
  287.2 28.2 %collective-permute-start.1 = (f32[256,512]{1,0:T(8,128)}, f32[256,512]{1,0:T(8,128)S(1)}, u32[]{:S(2)}, u32[]{:S(2)}) collective-permute-start(f32[256,512]{1,0:T(8,128)} %get-tuple-element.35), channel_id=1, source_target_pairs={{0,16},{8,24},{16,0},{24,8},{1,17},{9,25},{17,1},{25,9},{2,18},{10... | collective-permute-start | bytes 1572872 | tf_op jit(solution)/shard_map/ppermute | solution.py:49
  288.7 26.7 %collective-permute-start.2 = (f32[256,512]{1,0:T(8,128)}, f32[256,512]{1,0:T(8,128)S(1)}, u32[]{:S(2)}, u32[]{:S(2)}) collective-permute-start(f32[256,512]{1,0:T(8,128)} %get-tuple-element.36), channel_id=1, source_target_pairs={{0,24},{8,16},{16,8},{24,0},{1,25},{9,17},{17,9},{25,1},{2,26},{10... | collective-permute-start | bytes 1572872 | tf_op jit(solution)/shard_map/ppermute | solution.py:49
  315.4 0.8 copy-start.18
  315.4 1.0 copy-start.19
  315.4 1.1 copy-start.20
  321.8 24.8 %copy-start.25 = (f32[256,512]{1,0:T(8,128)S(1)}, f32[256,512]{1,0:T(8,128)}, u32[]{:S(2)}) copy-start(f32[256,512]{1,0:T(8,128)} %get-tuple-element.49) | copy-start | bytes 1572868
  321.8 26.3 %copy-start.24 = (f32[256,512]{1,0:T(8,128)S(1)}, f32[256,512]{1,0:T(8,128)}, u32[]{:S(2)}) copy-start(f32[256,512]{1,0:T(8,128)} %get-tuple-element.50) | copy-start | bytes 1572868
  341.4 52.6 %all-to-all-start.2 = ((f32[8,128,512]{2,1,0:T(8,128)}), f32[8,128,512]{2,1,0:T(8,128)S(1)}, u32[]{:S(2)}, u32[]{:S(2)}) async-start(f32[8,128,512]{2,1,0:T(8,128)} %negative_sums.4.refs_4_), calls=%async_computation.2 | async-start | bytes 4194304 | tf_op jit(solution)/shard_map/all_to_all | solution.py:465
  345.0 15.0 %collective-permute-start.9 = (f32[256,512]{1,0:T(8,128)}, f32[256,512]{1,0:T(8,128)S(1)}, u32[]{:S(2)}, u32[]{:S(2)}) collective-permute-start(f32[256,512]{1,0:T(8,128)} %get-tuple-element.48), channel_id=1, source_target_pairs={{0,8},{8,0},{16,24},{24,16},{1,9},{9,1},{17,25},{25,17},{2,10},{10... | collective-permute-start | bytes 1572872 | tf_op jit(solution)/shard_map/ppermute | solution.py:49
  346.6 24.1 %collective-permute-start.10 = (f32[256,512]{1,0:T(8,128)S(1)}, f32[256,512]{1,0:T(8,128)S(1)}, u32[]{:S(2)}, u32[]{:S(2)}) collective-permute-start(f32[256,512]{1,0:T(8,128)S(1)} %copy-done.25), channel_id=1, source_target_pairs={{0,16},{8,24},{16,0},{24,8},{1,17},{9,25},{17,1},{25,9},{2,18},{10... | collective-permute-start | bytes 1572872 | tf_op jit(solution)/shard_map/ppermute | solution.py:49
  348.1 23.6 %collective-permute-start.11 = (f32[256,512]{1,0:T(8,128)S(1)}, f32[256,512]{1,0:T(8,128)S(1)}, u32[]{:S(2)}, u32[]{:S(2)}) collective-permute-start(f32[256,512]{1,0:T(8,128)S(1)} %copy-done.24), channel_id=1, source_target_pairs={{0,24},{8,16},{16,8},{24,0},{1,25},{9,17},{17,9},{25,1},{2,26},{10... | collective-permute-start | bytes 1572872 | tf_op jit(solution)/shard_map/ppermute | solution.py:49
  360.0 11.7 %copy-start.15 = (f32[256,512]{1,0:T(8,128)}, f32[256,512]{1,0:T(8,128)S(1)}, u32[]{:S(2)}) copy-start(f32[256,512]{1,0:T(8,128)S(1)} %collective-permute-done.9.refs_1_) | copy-start | bytes 1572868
  370.7 1.0 copy-start.16
  371.7 0.8 copy-start.17
  394.0 3.5 copy-start.4
  394.0 18.8 %all-to-all-start.1 = ((f32[8,32,512]{2,1,0:T(8,128)}), f32[8,32,512]{2,1,0:T(8,128)S(1)}, u32[]{:S(2)}, u32[]{:S(2)}) async-start(f32[8,32,512]{2,1,0:T(8,128)} %negative_sums.6.refs_1_), calls=%async_computation.1 | async-start | bytes 1048576 | tf_op jit(solution)/shard_map/all_to_all | solution.py:465
  412.8 3.7 copy-start.8
  412.8 28.5 %all-to-all-start.4 = ((f32[4,256,512]{2,1,0:T(8,128)}), f32[4,256,512]{2,1,0:T(8,128)S(1)}, u32[]{:S(2)}, u32[]{:S(2)}) async-start(f32[4,256,512]{2,1,0:T(8,128)} %bitcast.107), calls=%async_computation.4 | async-start | bytes 4194304 | tf_op jit(solution)/shard_map/all_to_all | solution.py:470
  441.3 3.7 copy-start.3
  441.3 23.3 %all-to-all-start.3 = ((f32[4,128,512]{2,1,0:T(8,128)}), f32[4,128,512]{2,1,0:T(8,128)S(1)}, u32[]{:S(2)}, u32[]{:S(2)}) async-start(f32[4,128,512]{2,1,0:T(8,128)} %bitcast.109), calls=%async_computation.3 | async-start | bytes 2097152 | tf_op jit(solution)/shard_map/all_to_all | solution.py:470
  461.1 18.8 %collective-permute-start.14 = (f32[320,512]{1,0:T(8,128)}, f32[320,512]{1,0:T(8,128)S(1)}, u32[]{:S(2)}, u32[]{:S(2)}) collective-permute-start(f32[320,512]{1,0:T(8,128)} %inner_products.2.refs_2_.refs_0_), channel_id=1, source_target_pairs={{0,24},{8,16},{16,8},{24,0},{1,25},{9,17},{17,9},{25,1},{2,26},{10... | collective-permute-start | bytes 1966088 | tf_op jit(solution)/shard_map/ppermute | solution.py:49
  463.8 29.6 %collective-permute-start.13 = (f32[320,512]{1,0:T(8,128)}, f32[320,512]{1,0:T(8,128)S(1)}, u32[]{:S(2)}, u32[]{:S(2)}) collective-permute-start(f32[320,512]{1,0:T(8,128)} %inner_products.2.refs_2_.refs_0_), channel_id=1, source_target_pairs={{0,16},{8,24},{16,0},{24,8},{1,17},{9,25},{17,1},{25,9},{2,18},{10... | collective-permute-start | bytes 1966088 | tf_op jit(solution)/shard_map/ppermute | solution.py:49
  464.3 29.9 %collective-permute-start.12 = (f32[320,512]{1,0:T(8,128)}, f32[320,512]{1,0:T(8,128)S(1)}, u32[]{:S(2)}, u32[]{:S(2)}) collective-permute-start(f32[320,512]{1,0:T(8,128)} %inner_products.2.refs_2_.refs_0_), channel_id=1, source_target_pairs={{0,8},{8,0},{16,24},{24,16},{1,9},{9,1},{17,25},{25,17},{2,10},{10... | collective-permute-start | bytes 1966088 | tf_op jit(solution)/shard_map/ppermute | solution.py:49
  464.6 1.0 copy-start.7
  474.3 23.4 %collective-permute-start.17 = (f32[64,512]{1,0:T(8,128)}, f32[64,512]{1,0:T(8,128)S(1)}, u32[]{:S(2)}, u32[]{:S(2)}) collective-permute-start(f32[64,512]{1,0:T(8,128)} %inner_products.3.refs_4_.refs_1_), channel_id=1, source_target_pairs={{0,24},{8,16},{16,8},{24,0},{1,25},{9,17},{17,9},{25,1},{2,26},{10... | collective-permute-start | bytes 393224 | tf_op jit(solution)/shard_map/ppermute | solution.py:49
  477.0 20.7 %collective-permute-start.16 = (f32[64,512]{1,0:T(8,128)}, f32[64,512]{1,0:T(8,128)S(1)}, u32[]{:S(2)}, u32[]{:S(2)}) collective-permute-start(f32[64,512]{1,0:T(8,128)} %inner_products.3.refs_4_.refs_1_), channel_id=1, source_target_pairs={{0,16},{8,24},{16,0},{24,8},{1,17},{9,25},{17,1},{25,9},{2,18},{10... | collective-permute-start | bytes 393224 | tf_op jit(solution)/shard_map/ppermute | solution.py:49
  479.9 14.3 %copy-start.12 = (f32[320,512]{1,0:T(8,128)}, f32[320,512]{1,0:T(8,128)S(1)}, u32[]{:S(2)}) copy-start(f32[320,512]{1,0:T(8,128)S(1)} %collective-permute-done.14.refs_3_) | copy-start | bytes 1966084
  479.9 17.8 %collective-permute-start.15 = (f32[64,512]{1,0:T(8,128)}, f32[64,512]{1,0:T(8,128)S(1)}, u32[]{:S(2)}, u32[]{:S(2)}) collective-permute-start(f32[64,512]{1,0:T(8,128)} %inner_products.3.refs_4_.refs_1_), channel_id=1, source_target_pairs={{0,8},{8,0},{16,24},{24,16},{1,9},{9,1},{17,25},{25,17},{2,10},{10... | collective-permute-start | bytes 393224 | tf_op jit(solution)/shard_map/ppermute | solution.py:49
  493.4 0.8 copy-start.13
  494.2 0.8 copy-start.14
  497.7 0.6 copy-start.21
  497.7 0.7 copy-start.22
  497.8 0.7 copy-start.23
Sparse Core Ops, SparseCore 0:
  11.3 84.7 all-gather.3
  98.5 80.5 all-gather.5
  181.5 80.5 all-gather.7

commit v2 on v1

--- a/solution.py
+++ b/solution.py
@@ -184,7 +184,7 @@
             outs[i][...] = total_ref[...]
 
 
-def products(order, factor, inverse, first, last, pre=None, piece=(0, 1)):
+def products(order, factor, inverse, first, last, pre=None, piece=(0, 1), extra=()):
     with_split = factor.dtype == jnp.float32
     a_high, a_low = inverse
     count = last - first
@@ -226,6 +226,7 @@
         4 * length * part * count + 8 * rows * length,
         "products",
         scratch=[pltpu.VMEM((rows, part), jnp.float32)],
+        extra=extra,
     )
     if with_split:
         return got[0], list(got[1:])
@@ -295,55 +296,65 @@
     )
 
 
-def relay_kernel(*refs):
-    start = 0
-    for ref in refs[:-1]:
-        refs[-1][:, start : start + ref.shape[1], :] = ref[...]
-        start += ref.shape[1]
-
-
-def relay(order, *values):
+def relay_kernel(count, partner_ref, *refs):
+    outs = refs[count:]
+    ratio = outs[0].shape[0]
+    for s, out in enumerate(outs):
+        first = partner_ref[s] * ratio
+        for a in range(ratio):
+            start = 0
+            for ref in refs[:count]:
+                out[a, start : start + ref.shape[1], :] = ref[first + a]
+                start += ref.shape[1]
+
+
+def relay(order, partner, values):
     outer, _, width = values[0].shape
-    counts = [v.shape[1] for v in values]
-    half = outer // 2
-    return order(
-        relay_kernel,
+    pieces = partner.shape[0]
+    shape = (outer // pieces, sum(v.shape[1] for v in values), width)
+    return order(
+        functools.partial(relay_kernel, len(values)),
         list(values),
-        [pl.BlockSpec((half, n, width), lambda i: (i, 0, 0)) for n in counts],
-        shape_of((outer, sum(counts), width)),
-        pl.BlockSpec((half, sum(counts), width), lambda i: (i, 0, 0)),
-        (2,),
+        [pl.BlockSpec(v.shape, lambda i, p: (0, 0, 0)) for v in values],
+        [shape_of(shape)] * pieces,
+        [pl.BlockSpec(shape, lambda i, p: (0, 0, 0))] * pieces,
+        (1,),
         sum(v.size for v in values),
         8 * sum(v.size for v in values),
         "relay",
-    )
-
-
-def assembly_kernel(in_ref, *refs):
+        prefetch=[partner],
+    )
+
+
+def assembly_kernel(count, partner_ref, *refs):
     out_ref = refs[-1]
-    outer, inner, _, part = in_ref.shape
-    count = out_ref.shape[1]
-    for i in range(out_ref.shape[0]):
-        for a in range(inner):
-            for q in range(outer):
-                to = pl.ds((a * outer + q) * part, part)
-                out_ref[i, :, to] = in_ref[q, a, i * count : (i + 1) * count, :]
-
-
-def assembled(order, value, j, n, shape, whole=None):
-    operands = [value] + ([] if whole is None else [whole])
-    return order(
-        assembly_kernel,
+    ratio, _, part = refs[0].shape
+    for s in range(count):
+        for q in range(count):
+
+            @pl.when(partner_ref[s] == q)
+            def _():
+                for a in range(ratio):
+                    out_ref[0, :, pl.ds((a * count + q) * part, part)] = refs[s][a]
+
+
+def assembled(order, partner, values, j, shape, whole=None):
+    count = len(values)
+    operands = list(values) + ([] if whole is None else [whole])
+    size = count * values[0].size
+    return order(
+        functools.partial(assembly_kernel, count),
         operands,
-        [pl.BlockSpec(value.shape, lambda i: (0, 0, 0, 0))]
-        + [pl.BlockSpec(memory_space=pl.ANY)] * (len(operands) - 1),
+        [pl.BlockSpec(v.shape, lambda i, p: (0, 0, 0)) for v in values]
+        + [pl.BlockSpec(memory_space=pl.ANY)] * (len(operands) - count),
         shape_of(shape),
-        pl.BlockSpec((n, *shape[1:]), lambda i: (j, 0, 0)),
+        pl.BlockSpec((1, *shape[1:]), lambda i, p: (j, 0, 0)),
         (1,),
-        value.size,
-        8 * value.size,
+        size,
+        8 * size,
         "assembled",
-        aliases={} if whole is None else {1: 0},
+        prefetch=[partner],
+        aliases={} if whole is None else {1 + count: 0},
     )
 
 
@@ -464,11 +475,9 @@
     def to_columns(groups):
         return lax.all_to_all(negative_sums(order, groups, cols_n), "pcol", 0, 0)
 
-    def to_rows(value):
-        count = value.shape[1]
-        value = value.reshape(rows_n, ratio * count, part)
-        value = lax.all_to_all(value, "prow", 0, 0)
-        return value.reshape(rows_n, ratio, count, part)
+    def to_rows(*values):
+        pieces = relay(order, partner, values)
+        return [pieces[0]] + send(pieces[1:])
 
     def share(value):
         return [value] + [exchange(value, "prow", rows_n, s) for s in range(1, rows_n)]
@@ -513,21 +522,23 @@
     g2 = gather(shard)
     f1, sent = products(order, g1, inverse, 0, rows_n, pre1[0])
     s1 = [sent[0]] + send(sent[1:])
+    m0 = to_columns([s0])
     pre2 = elimination(
         order, [(c_two, f0), (c_three, f1)], [cols_n * (hi - lo) for lo, hi in last_cuts]
     )
 
-    f2, sent = products(order, g2, inverse, 0, rows_n, pre2[0], (0, 2))
+    f2, sent = products(order, g2, inverse, 0, rows_n, pre2[0], (0, 2), s1[1:])
     s2 = [sent[0]] + send(sent[1:])
-    m01 = to_columns([s0, s1])
-    f3, sent = products(order, g2, inverse, 1, rows_n, pre2[1], (1, 2))
-    s3 = send(sent)
+    m0 = to_rows(m0)
+    m1 = to_columns([s1])
+    f3, sent = products(order, g2, inverse, 0, rows_n, pre2[1], (1, 2))
+    s3 = [sent[0]] + send(sent[1:])
+    whole = assembled(order, partner, m0, 0, turned.shape)
     m2 = to_columns([s2])
-    _, own3 = products(order, f3, inverse, 0, 1)
-    m3 = to_columns([own3 + s3])
-    m01 = to_rows(relay(order, m01))
-    m23 = to_rows(relay(order, m2, m3))
-    whole = assembled(order, m01, 0, 2, turned.shape)
+    m1 = to_rows(m1)
+    m3 = to_columns([s3])
+    whole = assembled(order, partner, m1, 1, turned.shape, whole)
+    m23 = to_rows(m2, m3)
     columns_n, begin, pair = cols_n * local_cols, cols_n * cut, 2 * local_cols
     one = inner_products(
         order, whole, 0, 2, [f0, f1, f2, f3],
@@ -536,7 +547,7 @@
         (local_cols + 2 * pair, columns_n),
     )
     one = share(one)
-    whole = assembled(order, m23, 2, 1, turned.shape, whole)
+    whole = assembled(order, partner, m23, 2, turned.shape, whole)
     two = inner_products(
         order, whole, 2, 1, [f2, f3], [(0, c, local_cols) for c in (0, begin)],
         (local_cols, columns_n),

time: 510 us -> 530 us (1.039)
  blocking collectives: 19.6 us -> 0 us
  starting transfers between devices: 37.4 us -> 53.3 us
  Pallas kernels: 248 us -> 257 us
  waiting for transfers between devices: 158 us -> 166 us
    ppermute x18 -> x27, waiting for transfers between devices: 30.6 us -> 105 us  [exchange(): return lax.ppermute(value, axis, [(i, i ^ step) for i in range(size)])]
    all_to_all x2 -> x4, waiting for transfers between devices: 28.8 us -> 0.01 us  [to_columns(): return lax.all_to_all(negative_sums(order, groups, cols_n), 'pcol', 0, 0)]
    all_to_all x2 -> x0, waiting for transfers between devices: 22.7 us -> none  [to_rows(): value = lax.all_to_all(value, 'prow', 0, 0)]
    all_to_all x1 -> x0, blocking collectives: 19.6 us -> none  [to_columns(): return lax.all_to_all(negative_sums(order, groups, cols_n), 'pcol', 0, 0)]
    all_gather x3, waiting for transfers between devices: 75.4 us -> 60.6 us  [gather(): lax.all_gather(shard, 'pcol', axis=0, tiled=True)]
    ppermute x18 -> x27, starting transfers between devices: 22.6 us -> 34.5 us  [exchange(): return lax.ppermute(value, axis, [(i, i ^ step) for i in range(size)])]
    all_to_all x2 -> x4, starting transfers between devices: 7.1 us -> 18.5 us  [to_columns(): return lax.all_to_all(negative_sums(order, groups, cols_n), 'pcol', 0, 0)]
    pallas_call x22 -> x24, Pallas kernels: 248 us -> 257 us  [__call__(): pl.pallas_call(body, out_shape=out_shape, grid_spec=pltpu.PrefetchScalarG...]
  transfers between devices with their start and end apart: 25 -> 34, of which waited for: 12 -> 16; matrix products, arithmetic and copies ran while one was open for 5% -> 5% of each run, Pallas kernels for 46% -> 42%
where the time goes in v2:
time: 530 us; the launch traced here: 527 us
  Pallas kernels  257 us (48%)
  waiting for transfers between devices  166 us (31%)
  starting transfers between devices  53.3 us (10%)
  local copies, waits for them, and re-layouts  20.7 us (4%)
  between operations  14.1 us (3%)
  matrix products  10.5 us (2%)
  other arithmetic  5.59 us (1%)
    pallas_call x24, Pallas kernels, __call__(): pl.pallas_call(body, out_shape=out_shape, grid_spec=pltpu.PrefetchScalarG...  257 us
    ppermute x27, waiting for transfers between devices, exchange(): return lax.ppermute(value, axis, [(i, i ^ step) for i in range(size)])  105 us
    all_gather x3, waiting for transfers between devices, gather(): lax.all_gather(shard, 'pcol', axis=0, tiled=True)  60.6 us
    ppermute x27, starting transfers between devices, exchange(): return lax.ppermute(value, axis, [(i, i ^ step) for i in range(size)])  34.5 us
    all_to_all x4, starting transfers between devices, to_columns(): return lax.all_to_all(negative_sums(order, groups, cols_n), 'pcol', 0, 0)  18.5 us
    unnamed x107, local copies, waits for them, and re-layouts  17.7 us
  transfers between devices with their start and end apart: 34, of which 16 were waited for; matrix products, arithmetic and copies ran while one was open for 5% of the time, Pallas kernels for 42%

profile of v2, /device:TPU:0, one launch (start us, length us, event | category | flops | bytes accessed | tf_op | source)
XLA Modules:
  0.0 527.3 jit_solution(3510173681389533687)
XLA Ops:
  8.8 2.3 masked.3.refs_2_
  11.2 1.7 fusion.43
  12.9 2.5 copy.19
  15.5 2.6 copy.18
  18.0 2.5 copy.17
  21.1 28.8 %prepared.1 = (bf16[4,4096,512]{2,1,0:T(8,128)(2,1)}, bf16[4,4096,512]{2,1,0:T(8,128)(2,1)}) custom-call(s32[4]{0:T(128)} %iota_xor_fusion.refs_0_, f32[4096,2048]{1,0:T(8,128)} %refs_1_.1, f32[64,4096]{1,0:T(8,128)} %masked.3.refs_2_), custom_call_target="tpu_custom_call" | custom-call | flops 2097152 | bytes 4194304 | tf_op jit(solution)/shard_map/prepared/pallas_call | solution.py:64
  51.3 1.9 convolution_subtract_fusion
  63.8 1.6 pad_maximum_fusion
  65.4 30.7 %all-gather.4.cloned.1.call-done = f32[512,4096]{1,0:T(8,128)} async-done(((f32[64,4096]{1,0:T(8,128)}), f32[512,4096]{1,0:T(8,128)}) %all-gather.4.cloned.1.call-update) | async-done | bytes 8388624 | tf_op jit(solution)/shard_map/all_gather | solution.py:470
  96.0 2.3 masked.4.refs_3_
  98.6 38.1 %products.4 = (bf16[1024,4096]{1,0:T(8,128)(2,1)}, f32[512,512]{1,0:T(8,128)}, f32[512,512]{1,0:T(8,128)}, f32[512,512]{1,0:T(8,128)}, f32[512,512]{1,0:T(8,128)}) custom-call(f32[8,64,4096]{2,1,0:T(8,128)} %bitcast.99, bf16[4,4096,512]{2,1,0:T(8,128)(2,1)} %get-tuple-element.41.refs_8_.refs_1_.refs_2_, ...), custom_call_target="tpu_custom_call" | custom-call | flops 1610612736 | bytes 3145728 | tf_op jit(solution)/shard_map/products/pallas_call | solution.py:64
  136.7 12.5 %elimination.2.refs_3_.refs_1_ = f32[512,4096]{1,0:T(8,128)} custom-call(bf16[1024,512]{1,0:T(8,128)(2,1)} %get-tuple-element.95.refs_3_.refs_0_, bf16[1024,4096]{1,0:T(8,128)(2,1)} %get-tuple-element.43.refs_1_.refs_2_, bf16[1024,4096]{1,0:T(8,128)(2,1)} %get-tuple-element.43.refs_1_.refs_2_), custom_call_target="tpu_custom_call" | custom-call | flops 402653184 | bytes 1048576 | tf_op jit(solution)/shard_map/elimination/pallas_call | solution.py:64
  149.2 29.9 %all-gather.6.cloned.1.call-done = f32[512,4096]{1,0:T(8,128)} async-done(((f32[64,4096]{1,0:T(8,128)}), f32[512,4096]{1,0:T(8,128)}) %all-gather.6.cloned.1.call-update) | async-done | bytes 8388624 | tf_op jit(solution)/shard_map/all_gather | solution.py:470
  179.1 2.4 masked.5.refs_4_
  181.6 1.6 collective-permute-start
  183.1 1.5 collective-permute-start.1
  185.1 41.0 %products.5 = (bf16[1024,4096]{1,0:T(8,128)(2,1)}, f32[512,512]{1,0:T(8,128)}, f32[512,512]{1,0:T(8,128)}, f32[512,512]{1,0:T(8,128)}, f32[512,512]{1,0:T(8,128)}) custom-call(f32[8,64,4096]{2,1,0:T(8,128)} %bitcast.95, f32[512,4096]{1,0:T(8,128)} %elimination.2.refs_3_.refs_1_, bf16[4,4096,512]{2,1,0:T(8,128)(2,1)} %get-tuple-element.41.refs_8_.refs_1_.refs_2_, ...), custom_call_target="tpu_custom_call" | custom-call | flops 1610612736 | bytes 3145728 | tf_op jit(solution)/shard_map/products/pallas_call | solution.py:64
  226.1 4.5 collective-permute-done.1.refs_2_
  232.0 5.9 %negative_sums.5.refs_4_ = f32[8,64,512]{2,1,0:T(8,128)} custom-call(f32[512,512]{1,0:T(8,128)} %get-tuple-element.45.refs_0_, f32[512,512]{1,0:T(8,128)} %copy-done.11, f32[512,512]{1,0:T(8,128)} %copy-done.12, f32[512,512]{1,0:T(8,128)} %copy-done.13, bf16[1024,4096]{1,0:T(8,128)(2,1)} %get-tuple-element.44.refs_4_.refs_3_.refs_2_), custom_call_target="tpu_custom_call" | custom-call | flops 65536 | bytes 262144 | tf_op jit(solution)/shard_map/negative_sums/pallas_call | solution.py:64
  237.9 4.2 all-to-all-start
  244.3 1.5 collective-permute-start.5
  245.8 17.7 %elimination.3 = (f32[256,4096]{1,0:T(8,128)}, f32[256,4096]{1,0:T(8,128)}) custom-call(bf16[1024,512]{1,0:T(8,128)(2,1)} %get-tuple-element.96.refs_4_.refs_0_, bf16[1024,4096]{1,0:T(8,128)(2,1)} %get-tuple-element.43.refs_1_.refs_2_, bf16[1024,512]{1,0:T(8,128)(2,1)} %pad_maximum_fusion.2.refs_5_.refs_2_, ...), custom_call_target="tpu_custom_call" | custom-call | flops 805306368 | bytes 1572864 | tf_op jit(solution)/shard_map/elimination/pallas_call | solution.py:64
  263.5 5.0 collective-permute-done.3.refs_4_.refs_1_
  268.6 22.7 %collective-permute-done.5.refs_6_.refs_3_ = f32[512,512]{1,0:T(8,128)S(1)} collective-permute-done((f32[512,512]{1,0:T(8,128)}, f32[512,512]{1,0:T(8,128)S(1)}, u32[]{:S(2)}, u32[]{:S(2)}) %collective-permute-start.5) | collective-permute-done | bytes 1048608 | tf_op jit(solution)/shard_map/ppermute | solution.py:49
  292.2 23.5 %products.6 = (bf16[512,4096]{1,0:T(8,128)(2,1)}, f32[256,512]{1,0:T(8,128)}, f32[256,512]{1,0:T(8,128)}, f32[256,512]{1,0:T(8,128)}, f32[256,512]{1,0:T(8,128)}) custom-call(f32[8,64,4096]{2,1,0:T(8,128)} %bitcast.96, f32[256,4096]{1,0:T(8,128)} %get-tuple-element.49.refs_1_.refs_7_, bf16[4,4096,512]{2,1,0:T(8,128)(2,1)} %get-tuple-element.41.refs_8_.refs_1_.refs_2_, ...), custom_call_target="tpu_custom_call" | custom-call | flops 805306368 | bytes 2621440 | tf_op jit(solution)/shard_map/products/pallas_call | solution.py:64
  315.7 2.9 relay.3
  318.7 6.0 %negative_sums.6.refs_4_ = f32[8,64,512]{2,1,0:T(8,128)} custom-call(f32[512,512]{1,0:T(8,128)} %get-tuple-element.63.refs_0_, f32[512,512]{1,0:T(8,128)} %copy-done.6, f32[512,512]{1,0:T(8,128)} %copy-done.7, f32[512,512]{1,0:T(8,128)} %copy-done.8, f32[2,64,512]{2,1,0:T(8,128)} %get-tuple-element.58.refs_4_.refs_1_), custom_call_target="tpu_custom_call" | custom-call | flops 65536 | bytes 262144 | tf_op jit(solution)/shard_map/negative_sums/pallas_call | solution.py:64
  324.7 4.8 all-to-all-start.2
  329.5 1.3 collective-permute-start.9
  332.8 1.5 collective-permute-start.8
  334.3 1.5 collective-permute-start.10
  335.7 2.9 collective-permute-done.9.refs_2_
  338.7 2.1 collective-permute-start.11
  340.8 23.3 %products.7 = (bf16[512,4096]{1,0:T(8,128)(2,1)}, f32[256,512]{1,0:T(8,128)}, f32[256,512]{1,0:T(8,128)}, f32[256,512]{1,0:T(8,128)}, f32[256,512]{1,0:T(8,128)}) custom-call(f32[8,64,4096]{2,1,0:T(8,128)} %bitcast.97, f32[256,4096]{1,0:T(8,128)} %get-tuple-element.62.refs_1_, bf16[4,4096,512]{2,1,0:T(8,128)(2,1)} %get-tuple-element.41.refs_8_.refs_1_.refs_2_, ...), custom_call_target="tpu_custom_call" | custom-call | flops 805306368 | bytes 2621440 | tf_op jit(solution)/shard_map/products/pallas_call | solution.py:64
  364.1 3.7 collective-permute-done.10.refs_3_
  368.6 3.0 assembled.3.refs_4_.refs_5_
  372.7 5.4 %negative_sums.7.refs_2_ = f32[8,32,512]{2,1,0:T(8,128)} custom-call(f32[256,512]{1,0:T(8,128)} %get-tuple-element.53.refs_0_, f32[256,512]{1,0:T(8,128)} %copy-done.20, f32[256,512]{1,0:T(8,128)} %copy-done.21, f32[256,512]{1,0:T(8,128)} %copy-done.22, f32[3,64,4096]{2,1,0:T(8,128)} %assembled.3.refs_4_.refs_5_), custom_call_target="tpu_custom_call" | custom-call | flops 32768 | bytes 131072 | tf_op jit(solution)/shard_map/negative_sums/pallas_call | solution.py:64
  378.1 4.8 all-to-all-start.1
  382.9 1.3 collective-permute-start.12
  384.1 1.5 collective-permute-start.13
  386.4 2.9 relay.4
  389.3 8.3 %collective-permute-done.12.refs_1_ = f32[256,512]{1,0:T(8,128)S(1)} collective-permute-done((f32[256,512]{1,0:T(8,128)S(1)}, f32[256,512]{1,0:T(8,128)S(1)}, u32[]{:S(2)}, u32[]{:S(2)}) %collective-permute-start.12) | collective-permute-done | bytes 524320 | tf_op jit(solution)/shard_map/ppermute | solution.py:49
  397.7 11.7 %collective-permute-done.13.refs_2_ = f32[256,512]{1,0:T(8,128)S(1)} collective-permute-done((f32[256,512]{1,0:T(8,128)S(1)}, f32[256,512]{1,0:T(8,128)S(1)}, u32[]{:S(2)}, u32[]{:S(2)}) %collective-permute-start.13) | collective-permute-done | bytes 524320 | tf_op jit(solution)/shard_map/ppermute | solution.py:49
  410.4 5.2 negative_sums.8.refs_6_
  415.6 4.8 all-to-all-start.3
  422.4 1.5 collective-permute-start.17
  423.9 5.8 %collective-permute-done.15.refs_2_ = f32[2,64,512]{2,1,0:T(8,128)S(1)} collective-permute-done((f32[2,64,512]{2,1,0:T(8,128)}, f32[2,64,512]{2,1,0:T(8,128)S(1)}, u32[]{:S(2)}, u32[]{:S(2)}) %collective-permute-start.15) | collective-permute-done | bytes 262176 | tf_op jit(solution)/shard_map/ppermute | solution.py:49
  429.8 6.0 %collective-permute-done.17.refs_4_ = f32[2,64,512]{2,1,0:T(8,128)S(1)} collective-permute-done((f32[2,64,512]{2,1,0:T(8,128)S(1)}, f32[2,64,512]{2,1,0:T(8,128)S(1)}, u32[]{:S(2)}, u32[]{:S(2)}) %collective-permute-start.17) | collective-permute-done | bytes 262176 | tf_op jit(solution)/shard_map/ppermute | solution.py:49
  436.5 3.2 assembled.4.refs_3_.refs_0_.refs_5_
  440.5 2.9 relay.5
  443.4 13.1 %inner_products.2.refs_6_.refs_0_ = f32[320,512]{1,0:T(8,128)} custom-call(f32[3,64,4096]{2,1,0:T(8,128)} %assembled.4.refs_3_.refs_0_.refs_5_, bf16[1024,4096]{1,0:T(8,128)(2,1)} %get-tuple-element.43.refs_1_.refs_2_, bf16[1024,4096]{1,0:T(8,128)(2,1)} %get-tuple-element.44.refs_4_.refs_3_.refs_2_, ...), custom_call_target="tpu_custom_call" | custom-call | flops 251658240 | bytes 1572864 | tf_op jit(solution)/shard_map/inner_products/pallas_call | solution.py:64
  456.5 2.2 collective-permute-start.23
  458.7 1.3 collective-permute-start.22
  460.0 1.3 collective-permute-start.21
  461.3 1.5 collective-permute-start.19
  462.8 17.3 %collective-permute-done.18.refs_2_ = f32[2,64,512]{2,1,0:T(8,128)S(1)} collective-permute-done((f32[2,64,512]{2,1,0:T(8,128)S(1)}, f32[2,64,512]{2,1,0:T(8,128)S(1)}, u32[]{:S(2)}, u32[]{:S(2)}) %collective-permute-start.18) | collective-permute-done | bytes 262176 | tf_op jit(solution)/shard_map/ppermute | solution.py:49
  480.0 2.2 collective-permute-start.20
  482.3 12.6 %collective-permute-done.19.refs_3_ = f32[2,64,512]{2,1,0:T(8,128)S(1)} collective-permute-done((f32[2,64,512]{2,1,0:T(8,128)S(1)}, f32[2,64,512]{2,1,0:T(8,128)S(1)}, u32[]{:S(2)}, u32[]{:S(2)}) %collective-permute-start.19) | collective-permute-done | bytes 262176 | tf_op jit(solution)/shard_map/ppermute | solution.py:49
  494.9 4.4 collective-permute-done.20.refs_4_
  500.0 3.0 assembled.5.refs_0_.refs_3_
  503.0 6.5 %inner_products.3.refs_4_.refs_1_ = f32[64,512]{1,0:T(8,128)} custom-call(f32[3,64,4096]{2,1,0:T(8,128)} %assembled.5.refs_0_.refs_3_, bf16[512,4096]{1,0:T(8,128)(2,1)} %get-tuple-element.57.refs_2_.refs_3_.refs_1_, bf16[512,4096]{1,0:T(8,128)(2,1)} %get-tuple-element.64.refs_5_.refs_4_.refs_2_, f32[3,64,4096]{2,1,0:T(8,128)} %assembled.5.refs_0_.refs_3_), custom_call_target="tpu_custom_call" | custom-call | flops 50331648 | bytes 524288 | tf_op jit(solution)/shard_map/inner_products/pallas_call | solution.py:64
  511.5 1.5 collective-permute-start.24
  514.7 2.6 negative_sums.9.refs_7_
  518.0 2.7 finish.1
  (163 shorter events, 33.9 us)
Async XLA Ops:
  7.2 4.0 copy-start
  7.2 88.9 %all-gather.4.cloned.1.call-start = ((), (), s32[]{:S(2)}) async-start(), calls=%async_computation.4 | async-start | bytes 9437184 | tf_op jit(solution)/shard_map/all_gather | solution.py:470
  11.1 168.0 %all-gather.6.cloned.1.call-start = ((), (), s32[]{:S(2)}) async-start(), calls=%async_computation.5 | async-start | bytes 9437184 | tf_op jit(solution)/shard_map/all_gather | solution.py:470
  21.1 28.8 %copy-start.1 = (f32[3,512,512]{2,1,0:T(8,128)S(1)}, f32[3,512,512]{2,1,0:T(8,128)}, u32[]{:S(2)}) copy-start(f32[3,512,512]{2,1,0:T(8,128)} %param.9) | copy-start | bytes 9437188
  54.3 4.1 copy-start.4
  98.3 192.9 %all-gather.8.cloned.1.call-start = ((), (), s32[]{:S(2)}) async-start(), calls=%async_computation.6 | async-start | bytes 9437184 | tf_op jit(solution)/shard_map/all_gather | solution.py:470
  179.1 4.0 copy-start.36
  179.1 5.5 %copy-start.35 = (f32[512,512]{1,0:T(8,128)S(1)}, f32[512,512]{1,0:T(8,128)}, u32[]{:S(2)}) copy-start(f32[512,512]{1,0:T(8,128)} %get-tuple-element.48) | copy-start | bytes 3145732
  181.6 44.5 %collective-permute-start = (f32[512,512]{1,0:T(8,128)S(1)}, f32[512,512]{1,0:T(8,128)S(1)}, u32[]{:S(2)}, u32[]{:S(2)}) collective-permute-start(f32[512,512]{1,0:T(8,128)S(1)} %copy-done.37), channel_id=1, source_target_pairs={{0,8},{8,0},{16,24},{24,16},{1,9},{9,1},{17,25},{25,17},{2,10},{10... | collective-permute-start | bytes 3145736 | tf_op jit(solution)/shard_map/ppermute | solution.py:49
  183.1 47.5 %collective-permute-start.1 = (f32[512,512]{1,0:T(8,128)S(1)}, f32[512,512]{1,0:T(8,128)S(1)}, u32[]{:S(2)}, u32[]{:S(2)}) collective-permute-start(f32[512,512]{1,0:T(8,128)S(1)} %copy-done.36), channel_id=1, source_target_pairs={{0,16},{8,24},{16,0},{24,8},{1,17},{9,25},{17,1},{25,9},{2,18},{10... | collective-permute-start | bytes 3145736 | tf_op jit(solution)/shard_map/ppermute | solution.py:49
  184.6 46.0 %collective-permute-start.2 = (f32[512,512]{1,0:T(8,128)S(1)}, f32[512,512]{1,0:T(8,128)S(1)}, u32[]{:S(2)}, u32[]{:S(2)}) collective-permute-start(f32[512,512]{1,0:T(8,128)S(1)} %copy-done.35), channel_id=1, source_target_pairs={{0,24},{8,16},{16,8},{24,0},{1,25},{9,17},{17,9},{25,1},{2,26},{10... | collective-permute-start | bytes 3145736 | tf_op jit(solution)/shard_map/ppermute | solution.py:49
  226.1 4.5 copy-start.11
  237.9 77.8 %all-to-all-start = ((f32[8,64,512]{2,1,0:T(8,128)}), f32[8,64,512]{2,1,0:T(8,128)}, u32[]{:S(2)}, u32[]{:S(2)}) async-start(f32[8,64,512]{2,1,0:T(8,128)} %negative_sums.5.refs_4_), calls=%async_computation | async-start | bytes 2097152 | tf_op jit(solution)/shard_map/all_to_all | solution.py:476
  242.2 26.3 %collective-permute-start.3 = (f32[512,512]{1,0:T(8,128)}, f32[512,512]{1,0:T(8,128)S(1)}, u32[]{:S(2)}, u32[]{:S(2)}) collective-permute-start(f32[512,512]{1,0:T(8,128)} %get-tuple-element.50), channel_id=1, source_target_pairs={{0,8},{8,0},{16,24},{24,16},{1,9},{9,1},{17,25},{25,17},{2,10},{10... | collective-permute-start | bytes 3145736 | tf_op jit(solution)/shard_map/ppermute | solution.py:49
  243.1 25.5 %collective-permute-start.4 = (f32[512,512]{1,0:T(8,128)}, f32[512,512]{1,0:T(8,128)S(1)}, u32[]{:S(2)}, u32[]{:S(2)}) collective-permute-start(f32[512,512]{1,0:T(8,128)} %get-tuple-element.51), channel_id=1, source_target_pairs={{0,16},{8,24},{16,0},{24,8},{1,17},{9,25},{17,1},{25,9},{2,18},{10... | collective-permute-start | bytes 3145736 | tf_op jit(solution)/shard_map/ppermute | solution.py:49
  244.3 47.0 %collective-permute-start.5 = (f32[512,512]{1,0:T(8,128)}, f32[512,512]{1,0:T(8,128)S(1)}, u32[]{:S(2)}, u32[]{:S(2)}) collective-permute-start(f32[512,512]{1,0:T(8,128)} %get-tuple-element.52), channel_id=1, source_target_pairs={{0,24},{8,16},{16,8},{24,0},{1,25},{9,17},{17,9},{25,1},{2,26},{10... | collective-permute-start | bytes 3145736 | tf_op jit(solution)/shard_map/ppermute | solution.py:49
  268.5 22.8 %copy-start.6 = (f32[512,512]{1,0:T(8,128)}, f32[512,512]{1,0:T(8,128)S(1)}, u32[]{:S(2)}) copy-start(f32[512,512]{1,0:T(8,128)S(1)} %collective-permute-done.3.refs_4_.refs_1_) | copy-start | bytes 3145732
  268.6 22.7 %copy-start.7 = (f32[512,512]{1,0:T(8,128)}, f32[512,512]{1,0:T(8,128)S(1)}, u32[]{:S(2)}) copy-start(f32[512,512]{1,0:T(8,128)S(1)} %collective-permute-done.4.refs_5_.refs_2_) | copy-start | bytes 3145732
  318.6 10.8 %copy-start.49 = (f32[2,64,512]{2,1,0:T(8,128)S(1)}, f32[2,64,512]{2,1,0:T(8,128)}, u32[]{:S(2)}) copy-start(f32[2,64,512]{2,1,0:T(8,128)} %get-tuple-element.59) | copy-start | bytes 786436
  318.6 12.1 %copy-start.40 = (f32[256,512]{1,0:T(8,128)S(1)}, f32[256,512]{1,0:T(8,128)}, u32[]{:S(2)}) copy-start(f32[256,512]{1,0:T(8,128)} %get-tuple-element.54) | copy-start | bytes 1572868
  318.7 12.9 %copy-start.39 = (f32[256,512]{1,0:T(8,128)S(1)}, f32[256,512]{1,0:T(8,128)}, u32[]{:S(2)}) copy-start(f32[256,512]{1,0:T(8,128)} %get-tuple-element.55) | copy-start | bytes 1572868
  318.7 14.1 %copy-start.38 = (f32[256,512]{1,0:T(8,128)S(1)}, f32[256,512]{1,0:T(8,128)}, u32[]{:S(2)}) copy-start(f32[256,512]{1,0:T(8,128)} %get-tuple-element.56) | copy-start | bytes 1572868
  318.7 15.6 %copy-start.45 = (f32[2,64,512]{2,1,0:T(8,128)S(1)}, f32[2,64,512]{2,1,0:T(8,128)}, u32[]{:S(2)}) copy-start(f32[2,64,512]{2,1,0:T(8,128)} %get-tuple-element.60) | copy-start | bytes 786436
  318.7 20.0 %copy-start.44 = (f32[2,64,512]{2,1,0:T(8,128)S(1)}, f32[2,64,512]{2,1,0:T(8,128)}, u32[]{:S(2)}) copy-start(f32[2,64,512]{2,1,0:T(8,128)} %get-tuple-element.61) | copy-start | bytes 786436
  324.7 53.4 %all-to-all-start.2 = ((f32[8,64,512]{2,1,0:T(8,128)}), f32[8,64,512]{2,1,0:T(8,128)S(1)}, u32[]{:S(2)}, u32[]{:S(2)}) async-start(f32[8,64,512]{2,1,0:T(8,128)} %negative_sums.6.refs_4_), calls=%async_computation.2 | async-start | bytes 2097152 | tf_op jit(solution)/shard_map/all_to_all | solution.py:476
  329.5 9.2 %collective-permute-start.9 = (f32[2,64,512]{2,1,0:T(8,128)S(1)}, f32[2,64,512]{2,1,0:T(8,128)S(1)}, u32[]{:S(2)}, u32[]{:S(2)}) collective-permute-start(f32[2,64,512]{2,1,0:T(8,128)S(1)} %copy-done.49), channel_id=1, source_target_pairs={{0,8},{8,0},{16,24},{24,16},{1,9},{9,1},{17,25},{25,17},{2,10},{10... | collective-permute-start | bytes 786440 | tf_op jit(solution)/shard_map/ppermute | solution.py:49
  330.8 40.8 %collective-permute-start.6 = (f32[256,512]{1,0:T(8,128)S(1)}, f32[256,512]{1,0:T(8,128)S(1)}, u32[]{:S(2)}, u32[]{:S(2)}) collective-permute-start(f32[256,512]{1,0:T(8,128)S(1)} %copy-done.40), channel_id=1, source_target_pairs={{0,8},{8,0},{16,24},{24,16},{1,9},{9,1},{17,25},{25,17},{2,10},{10... | collective-permute-start | bytes 1572872 | tf_op jit(solution)/shard_map/ppermute | solution.py:49
  331.6 40.0 %collective-permute-start.7 = (f32[256,512]{1,0:T(8,128)S(1)}, f32[256,512]{1,0:T(8,128)S(1)}, u32[]{:S(2)}, u32[]{:S(2)}) collective-permute-start(f32[256,512]{1,0:T(8,128)S(1)} %copy-done.39), channel_id=1, source_target_pairs={{0,16},{8,24},{16,0},{24,8},{1,17},{9,25},{17,1},{25,9},{2,18},{10... | collective-permute-start | bytes 1572872 | tf_op jit(solution)/shard_map/ppermute | solution.py:49
  332.8 38.8 %collective-permute-start.8 = (f32[256,512]{1,0:T(8,128)S(1)}, f32[256,512]{1,0:T(8,128)S(1)}, u32[]{:S(2)}, u32[]{:S(2)}) collective-permute-start(f32[256,512]{1,0:T(8,128)S(1)} %copy-done.38), channel_id=1, source_target_pairs={{0,24},{8,16},{16,8},{24,0},{1,25},{9,17},{17,9},{25,1},{2,26},{10... | collective-permute-start | bytes 1572872 | tf_op jit(solution)/shard_map/ppermute | solution.py:49
  334.3 33.5 %collective-permute-start.10 = (f32[2,64,512]{2,1,0:T(8,128)S(1)}, f32[2,64,512]{2,1,0:T(8,128)S(1)}, u32[]{:S(2)}, u32[]{:S(2)}) collective-permute-start(f32[2,64,512]{2,1,0:T(8,128)S(1)} %copy-done.45), channel_id=1, source_target_pairs={{0,16},{8,24},{16,0},{24,8},{1,17},{9,25},{17,1},{25,9},{2,18},{10... | collective-permute-start | bytes 786440 | tf_op jit(solution)/shard_map/ppermute | solution.py:49
  338.7 25.4 %copy-start.23 = (f32[2,64,512]{2,1,0:T(8,128)}, f32[2,64,512]{2,1,0:T(8,128)S(1)}, u32[]{:S(2)}) copy-start(f32[2,64,512]{2,1,0:T(8,128)S(1)} %collective-permute-done.9.refs_2_) | copy-start | bytes 786436
  338.7 29.1 %collective-permute-start.11 = (f32[2,64,512]{2,1,0:T(8,128)S(1)}, f32[2,64,512]{2,1,0:T(8,128)S(1)}, u32[]{:S(2)}, u32[]{:S(2)}) collective-permute-start(f32[2,64,512]{2,1,0:T(8,128)S(1)} %copy-done.44), channel_id=1, source_target_pairs={{0,24},{8,16},{16,8},{24,0},{1,25},{9,17},{17,9},{25,1},{2,26},{10... | collective-permute-start | bytes 786440 | tf_op jit(solution)/shard_map/ppermute | solution.py:49
  372.7 10.1 %copy-start.43 = (f32[256,512]{1,0:T(8,128)S(1)}, f32[256,512]{1,0:T(8,128)}, u32[]{:S(2)}) copy-start(f32[256,512]{1,0:T(8,128)} %get-tuple-element.66) | copy-start | bytes 1572868
  372.7 11.4 %copy-start.42 = (f32[256,512]{1,0:T(8,128)S(1)}, f32[256,512]{1,0:T(8,128)}, u32[]{:S(2)}) copy-start(f32[256,512]{1,0:T(8,128)} %get-tuple-element.67) | copy-start | bytes 1572868
  372.7 12.9 %copy-start.41 = (f32[256,512]{1,0:T(8,128)S(1)}, f32[256,512]{1,0:T(8,128)}, u32[]{:S(2)}) copy-start(f32[256,512]{1,0:T(8,128)} %get-tuple-element.68) | copy-start | bytes 1572868
  378.1 8.3 %copy-start.5 = (f32[8,64,512]{2,1,0:T(8,128)}, f32[8,64,512]{2,1,0:T(8,128)S(1)}, u32[]{:S(2)}) copy-start(f32[8,64,512]{2,1,0:T(8,128)S(1)} %all-to-all-done.2.refs_1_) | copy-start | bytes 3145732
  378.1 37.5 %all-to-all-start.1 = ((f32[8,32,512]{2,1,0:T(8,128)}), f32[8,32,512]{2,1,0:T(8,128)S(1)}, u32[]{:S(2)}, u32[]{:S(2)}) async-start(f32[8,32,512]{2,1,0:T(8,128)} %negative_sums.7.refs_2_), calls=%async_computation.1 | async-start | bytes 1048576 | tf_op jit(solution)/shard_map/all_to_all | solution.py:476
  382.9 14.8 %collective-permute-start.12 = (f32[256,512]{1,0:T(8,128)S(1)}, f32[256,512]{1,0:T(8,128)S(1)}, u32[]{:S(2)}, u32[]{:S(2)}) collective-permute-start(f32[256,512]{1,0:T(8,128)S(1)} %copy-done.43), channel_id=1, source_target_pairs={{0,8},{8,0},{16,24},{24,16},{1,9},{9,1},{17,25},{25,17},{2,10},{10... | collective-permute-start | bytes 1572872 | tf_op jit(solution)/shard_map/ppermute | solution.py:49
  384.1 25.2 %collective-permute-start.13 = (f32[256,512]{1,0:T(8,128)S(1)}, f32[256,512]{1,0:T(8,128)S(1)}, u32[]{:S(2)}, u32[]{:S(2)}) collective-permute-start(f32[256,512]{1,0:T(8,128)S(1)} %copy-done.42), channel_id=1, source_target_pairs={{0,16},{8,24},{16,0},{24,8},{1,17},{9,25},{17,1},{25,9},{2,18},{10... | collective-permute-start | bytes 1572872 | tf_op jit(solution)/shard_map/ppermute | solution.py:49
  385.6 23.8 %collective-permute-start.14 = (f32[256,512]{1,0:T(8,128)S(1)}, f32[256,512]{1,0:T(8,128)S(1)}, u32[]{:S(2)}, u32[]{:S(2)}) collective-permute-start(f32[256,512]{1,0:T(8,128)S(1)} %copy-done.41), channel_id=1, source_target_pairs={{0,24},{8,16},{16,8},{24,0},{1,25},{9,17},{17,9},{25,1},{2,26},{10... | collective-permute-start | bytes 1572872 | tf_op jit(solution)/shard_map/ppermute | solution.py:49
  389.3 33.0 %copy-start.46 = (f32[2,64,512]{2,1,0:T(8,128)S(1)}, f32[2,64,512]{2,1,0:T(8,128)}, u32[]{:S(2)}) copy-start(f32[2,64,512]{2,1,0:T(8,128)} %get-tuple-element.72) | copy-start | bytes 786436
  397.7 11.7 %copy-start.17 = (f32[256,512]{1,0:T(8,128)}, f32[256,512]{1,0:T(8,128)S(1)}, u32[]{:S(2)}) copy-start(f32[256,512]{1,0:T(8,128)S(1)} %collective-permute-done.12.refs_1_) | copy-start | bytes 1572868
  397.7 23.7 %copy-start.47 = (f32[2,64,512]{2,1,0:T(8,128)S(1)}, f32[2,64,512]{2,1,0:T(8,128)}, u32[]{:S(2)}) copy-start(f32[2,64,512]{2,1,0:T(8,128)} %get-tuple-element.71) | copy-start | bytes 786436
  415.6 24.1 %copy-start.9 = (f32[8,32,512]{2,1,0:T(8,128)}, f32[8,32,512]{2,1,0:T(8,128)S(1)}, u32[]{:S(2)}) copy-start(f32[8,32,512]{2,1,0:T(8,128)S(1)} %all-to-all-done.1.refs_1_) | copy-start | bytes 1572868
  415.6 24.1 %all-to-all-start.3 = ((f32[8,32,512]{2,1,0:T(8,128)}), f32[8,32,512]{2,1,0:T(8,128)S(1)}, u32[]{:S(2)}, u32[]{:S(2)}) async-start(f32[8,32,512]{2,1,0:T(8,128)} %negative_sums.8.refs_6_), calls=%async_computation.3 | async-start | bytes 1048576 | tf_op jit(solution)/shard_map/all_to_all | solution.py:476
  420.4 9.3 %collective-permute-start.15 = (f32[2,64,512]{2,1,0:T(8,128)}, f32[2,64,512]{2,1,0:T(8,128)S(1)}, u32[]{:S(2)}, u32[]{:S(2)}) collective-permute-start(f32[2,64,512]{2,1,0:T(8,128)} %get-tuple-element.70), channel_id=1, source_target_pairs={{0,8},{8,0},{16,24},{24,16},{1,9},{9,1},{17,25},{25,17},{2,10},{10... | collective-permute-start | bytes 786440 | tf_op jit(solution)/shard_map/ppermute | solution.py:49
  421.3 8.4 %collective-permute-start.16 = (f32[2,64,512]{2,1,0:T(8,128)S(1)}, f32[2,64,512]{2,1,0:T(8,128)S(1)}, u32[]{:S(2)}, u32[]{:S(2)}) collective-permute-start(f32[2,64,512]{2,1,0:T(8,128)S(1)} %copy-done.47), channel_id=1, source_target_pairs={{0,16},{8,24},{16,0},{24,8},{1,17},{9,25},{17,1},{25,9},{2,18},{10... | collective-permute-start | bytes 786440 | tf_op jit(solution)/shard_map/ppermute | solution.py:49
  422.4 13.4 %collective-permute-start.17 = (f32[2,64,512]{2,1,0:T(8,128)S(1)}, f32[2,64,512]{2,1,0:T(8,128)S(1)}, u32[]{:S(2)}, u32[]{:S(2)}) collective-permute-start(f32[2,64,512]{2,1,0:T(8,128)S(1)} %copy-done.46), channel_id=1, source_target_pairs={{0,24},{8,16},{16,8},{24,0},{1,25},{9,17},{17,9},{25,1},{2,26},{10... | collective-permute-start | bytes 786440 | tf_op jit(solution)/shard_map/ppermute | solution.py:49
  429.7 6.1 %copy-start.26 = (f32[2,64,512]{2,1,0:T(8,128)}, f32[2,64,512]{2,1,0:T(8,128)S(1)}, u32[]{:S(2)}) copy-start(f32[2,64,512]{2,1,0:T(8,128)S(1)} %collective-permute-done.15.refs_2_) | copy-start | bytes 786436
  429.8 6.0 %copy-start.29 = (f32[2,64,512]{2,1,0:T(8,128)}, f32[2,64,512]{2,1,0:T(8,128)S(1)}, u32[]{:S(2)}) copy-start(f32[2,64,512]{2,1,0:T(8,128)S(1)} %collective-permute-done.16.refs_3_) | copy-start | bytes 786436
  443.4 15.3 %copy-start.51 = (f32[2,64,512]{2,1,0:T(8,128)S(1)}, f32[2,64,512]{2,1,0:T(8,128)}, u32[]{:S(2)}) copy-start(f32[2,64,512]{2,1,0:T(8,128)} %get-tuple-element.74) | copy-start | bytes 786436
  443.4 17.9 %copy-start.50 = (f32[2,64,512]{2,1,0:T(8,128)S(1)}, f32[2,64,512]{2,1,0:T(8,128)}, u32[]{:S(2)}) copy-start(f32[2,64,512]{2,1,0:T(8,128)} %get-tuple-element.75) | copy-start | bytes 786436
  443.4 36.6 %copy-start.48 = (f32[2,64,512]{2,1,0:T(8,128)S(1)}, f32[2,64,512]{2,1,0:T(8,128)}, u32[]{:S(2)}) copy-start(f32[2,64,512]{2,1,0:T(8,128)} %get-tuple-element.76) | copy-start | bytes 786436
  456.5 55.0 %collective-permute-start.23 = (f32[320,512]{1,0:T(8,128)}, f32[320,512]{1,0:T(8,128)S(1)}, u32[]{:S(2)}, u32[]{:S(2)}) collective-permute-start(f32[320,512]{1,0:T(8,128)} %inner_products.2.refs_6_.refs_0_), channel_id=1, source_target_pairs={{0,24},{8,16},{16,8},{24,0},{1,25},{9,17},{17,9},{25,1},{2,26},{10... | collective-permute-start | bytes 1966088 | tf_op jit(solution)/shard_map/ppermute | solution.py:49
  458.7 21.3 %collective-permute-start.18 = (f32[2,64,512]{2,1,0:T(8,128)S(1)}, f32[2,64,512]{2,1,0:T(8,128)S(1)}, u32[]{:S(2)}, u32[]{:S(2)}) collective-permute-start(f32[2,64,512]{2,1,0:T(8,128)S(1)} %copy-done.51), channel_id=1, source_target_pairs={{0,8},{8,0},{16,24},{24,16},{1,9},{9,1},{17,25},{25,17},{2,10},{10... | collective-permute-start | bytes 786440 | tf_op jit(solution)/shard_map/ppermute | solution.py:49
  458.7 54.3 %collective-permute-start.22 = (f32[320,512]{1,0:T(8,128)}, f32[320,512]{1,0:T(8,128)S(1)}, u32[]{:S(2)}, u32[]{:S(2)}) collective-permute-start(f32[320,512]{1,0:T(8,128)} %inner_products.2.refs_6_.refs_0_), channel_id=1, source_target_pairs={{0,16},{8,24},{16,0},{24,8},{1,17},{9,25},{17,1},{25,9},{2,18},{10... | collective-permute-start | bytes 1966088 | tf_op jit(solution)/shard_map/ppermute | solution.py:49
  460.0 53.0 %collective-permute-start.21 = (f32[320,512]{1,0:T(8,128)}, f32[320,512]{1,0:T(8,128)S(1)}, u32[]{:S(2)}, u32[]{:S(2)}) collective-permute-start(f32[320,512]{1,0:T(8,128)} %inner_products.2.refs_6_.refs_0_), channel_id=1, source_target_pairs={{0,8},{8,0},{16,24},{24,16},{1,9},{9,1},{17,25},{25,17},{2,10},{10... | collective-permute-start | bytes 1966088 | tf_op jit(solution)/shard_map/ppermute | solution.py:49
  461.3 33.6 %collective-permute-start.19 = (f32[2,64,512]{2,1,0:T(8,128)S(1)}, f32[2,64,512]{2,1,0:T(8,128)S(1)}, u32[]{:S(2)}, u32[]{:S(2)}) collective-permute-start(f32[2,64,512]{2,1,0:T(8,128)S(1)} %copy-done.50), channel_id=1, source_target_pairs={{0,16},{8,24},{16,0},{24,8},{1,17},{9,25},{17,1},{25,9},{2,18},{10... | collective-permute-start | bytes 786440 | tf_op jit(solution)/shard_map/ppermute | solution.py:49
  480.0 19.3 %copy-start.24 = (f32[2,64,512]{2,1,0:T(8,128)}, f32[2,64,512]{2,1,0:T(8,128)S(1)}, u32[]{:S(2)}) copy-start(f32[2,64,512]{2,1,0:T(8,128)S(1)} %collective-permute-done.18.refs_2_) | copy-start | bytes 786436
  480.0 19.3 %collective-permute-start.20 = (f32[2,64,512]{2,1,0:T(8,128)S(1)}, f32[2,64,512]{2,1,0:T(8,128)S(1)}, u32[]{:S(2)}, u32[]{:S(2)}) collective-permute-start(f32[2,64,512]{2,1,0:T(8,128)S(1)} %copy-done.48), channel_id=1, source_target_pairs={{0,24},{8,16},{16,8},{24,0},{1,25},{9,17},{17,9},{25,1},{2,26},{10... | collective-permute-start | bytes 786440 | tf_op jit(solution)/shard_map/ppermute | solution.py:49
  494.9 4.4 copy-start.28
  509.5 7.8 %collective-permute-start.26 = (f32[64,512]{1,0:T(8,128)}, f32[64,512]{1,0:T(8,128)S(1)}, u32[]{:S(2)}, u32[]{:S(2)}) collective-permute-start(f32[64,512]{1,0:T(8,128)} %inner_products.3.refs_4_.refs_1_), channel_id=1, source_target_pairs={{0,24},{8,16},{16,8},{24,0},{1,25},{9,17},{17,9},{25,1},{2,26},{10... | collective-permute-start | bytes 393224 | tf_op jit(solution)/shard_map/ppermute | solution.py:49
  510.4 6.9 %collective-permute-start.25 = (f32[64,512]{1,0:T(8,128)}, f32[64,512]{1,0:T(8,128)S(1)}, u32[]{:S(2)}, u32[]{:S(2)}) collective-permute-start(f32[64,512]{1,0:T(8,128)} %inner_products.3.refs_4_.refs_1_), channel_id=1, source_target_pairs={{0,16},{8,24},{16,0},{24,8},{1,17},{9,25},{17,1},{25,9},{2,18},{10... | collective-permute-start | bytes 393224 | tf_op jit(solution)/shard_map/ppermute | solution.py:49
  511.5 5.8 %collective-permute-start.24 = (f32[64,512]{1,0:T(8,128)}, f32[64,512]{1,0:T(8,128)S(1)}, u32[]{:S(2)}, u32[]{:S(2)}) collective-permute-start(f32[64,512]{1,0:T(8,128)} %inner_products.3.refs_4_.refs_1_), channel_id=1, source_target_pairs={{0,8},{8,0},{16,24},{24,16},{1,9},{9,1},{17,25},{25,17},{2,10},{10... | collective-permute-start | bytes 393224 | tf_op jit(solution)/shard_map/ppermute | solution.py:49
  (22 other events, 24.7 us)
Sparse Core Ops, SparseCore 0:
  11.3 84.7 all-gather.3
  98.5 80.5 all-gather.5
  181.7 99.9 all-gather.7
